TPU v7x, 256 devices: a whole 4x4x8 slice. The times are simulated.
256 devices in a mesh: fsdp: 16 (over x_lo, z), st: 16 (over y, x_hi, core).
Axes of the slice: x: 4 (x_hi: 2, x_lo: 2; x = x_hi * 2 + x_lo), y: 4, z: 8, core: 2. Of those that a mesh axis runs over, the one named last changes fastest.
Arguments:
- queries: bfloat16 [1, 24576, 2048], P(None, 'st', 'fsdp'), may hold values from -4.5 to 4.5
- key_rows: bfloat16 [1, 24576, 2048], P(None, 'st', 'fsdp'), may hold values from -4.5 to 4.5
- value_rows: bfloat16 [1, 24576, 2048], P(None, 'st', 'fsdp'), may hold values from -6 to 6
- out_grad: bfloat16 [1, 24576, 1536], P(None, 'st', 'fsdp'), may hold values from -6 to 6
- proj_weight: bfloat16 [2048, 1536], P('fsdp'), may hold values from -0.125 to 0.125
- pattern: int32 [64, 27], P('st'), may hold values from -1 to 63, as said below
Outputs:
- projected: bfloat16 [1, 24576, 1536], P(None, 'st', 'fsdp')
- query_grad: bfloat16 [1, 24576, 2048], P(None, 'st', 'fsdp')
- key_grad: bfloat16 [1, 24576, 2048], P(None, 'st', 'fsdp')
- value_grad: bfloat16 [1, 24576, 2048], P(None, 'st', 'fsdp')
- weight_grad: float32 [2048, 1536], P('fsdp', 'st')
Inputs may be any that keep to these rules, and one draw needn't show every extreme that they name: Slot j stands for the offsets (j // 9 - 1) in frame, (j // 3 % 3 - 1) in tile row and (j % 3 - 1) in column; pattern[t, j] is -1 or the tile at t's frame, row and column plus those offsets, which lies inside the grid of 2 frames, 16 rows and 2 columns; slots 10, 13 and 16 are never -1 where that tile exists.
All inputs are finite; a program needn't handle non-finite values.
Results may differ from a plain program's by a relative error of at most 0.023.
Values may be sent and summed in bfloat16 or wider, within the bound.
No kernel may reach another device: no remote copies, remote signals or barrier semaphores. Data moves between devices by JAX's collectives and lax.ppermute only.
A program may use at most 128 MiB of HBM per device.

v0:
```python
import functools

import jax
import jax.numpy as jnp
from jax import lax
from jax.experimental import pallas as pl
from jax.experimental.pallas import tpu as pltpu
from jax.sharding import Mesh
from jax.sharding import PartitionSpec as P

HDIM = 128
TILE = 384
TF = 2
TC = 2
ROW_TILES = TF * TC
BAND = 3 * ROW_TILES
SCALING = HDIM ** (-0.5)
LOG2E = 1.4426950408889634
BF = jnp.bfloat16
F32 = jnp.float32
ST = ("y", "xh", "core")
NT = (((1,), (1,)), ((), ()))
TN = (((0,), (0,)), ((), ()))
NN = (((1,), (0,)), ((), ()))


def dot(a, b, dims):
    return lax.dot_general(a, b, dims, preferred_element_type=F32)


def build_pairs(pattern_ref, tile_of, place_of, rows):
    count = jnp.int32(0)
    for tile in range(ROW_TILES):
        frame, col = tile // TC, tile % TC
        for at, row in enumerate(rows):
            for inner in range(ROW_TILES):
                slot = (inner // TC - frame + 1) * 9 + row * 3 + (inner % TC - col + 1)
                tile_of[count] = jnp.int32(tile)
                place_of[count] = jnp.int32(at * ROW_TILES + inner)
                count = count + (pattern_ref[tile, slot] >= 0).astype(jnp.int32)
    return count


def run_pairs(count, make, use, even, odd):
    make(even, 0)

    def step(j, carry):
        i = 2 * j
        make(odd, i + 1)
        use(even, i)
        make(even, i + 2)
        use(odd, i + 1)
        return carry

    lax.fori_loop(0, (count - 1) // 2, step, 0)

    @pl.when(count % 2 == 1)
    def _():
        use(even, count - 1)

    @pl.when(count % 2 == 0)
    def _():
        make(odd, count - 1)
        use(even, count - 2)
        use(odd, count - 1)


def fill_band(refs, kband, vband, sem):
    copies = []
    for i, ref in enumerate(refs):
        place = pl.ds(i * ROW_TILES, ROW_TILES)
        copies.append(pltpu.make_async_copy(ref.at[0], kband.at[place], sem.at[2 * i]))
        copies.append(pltpu.make_async_copy(ref.at[1], vband.at[place], sem.at[2 * i + 1]))
    for copy in copies:
        copy.start()
    return copies


def forward_pairs(count, q_ref, kband, vband, tile_of, place_of, even, odd, top, total, acc):
    def make(slot, i):
        scores = dot(kband[place_of[i]], q_ref[tile_of[i]], NT) * (SCALING * LOG2E)
        slot[0][...] = scores
        slot[1][...] = jnp.max(scores, axis=0, keepdims=True)

    def use(slot, i):
        tile = tile_of[i]
        before = top[tile]
        peak = jnp.maximum(before, slot[1][...])
        shrink = jnp.exp2(before - peak)
        raised = jnp.exp2(slot[0][...] - peak)
        top[tile] = peak
        total[tile] = shrink * total[tile] + jnp.sum(raised, axis=0, keepdims=True)
        acc[tile] = shrink * acc[tile] + dot(vband[place_of[i]], raised.astype(BF), TN)

    run_pairs(count, make, use, even, odd)


def forward_own_kernel(
    pattern_ref, q_ref, k_ref, v_ref, top, total, acc, tile_of, place_of, s0, s1, m0, m1
):
    count = build_pairs(pattern_ref, tile_of, place_of, (1,))
    top[...] = jnp.full(top.shape, -jnp.inf, F32)
    total[...] = jnp.zeros(total.shape, F32)
    acc[...] = jnp.zeros(acc.shape, F32)
    forward_pairs(
        count, q_ref, k_ref, v_ref, tile_of, place_of, (s0, m0), (s1, m1), top, total, acc
    )


def forward_halo_kernel(
    pattern_ref, q_ref, top_in, total_in, acc_in, above_ref, below_ref, early_ref,
    att_ref, flip_ref, lse_ref,
    kband, vband, tile_of, place_of, s0, s1, m0, m1, top, total, acc, sem,
):
    copies = fill_band((above_ref, below_ref), kband, vband, sem)
    count = build_pairs(pattern_ref, tile_of, place_of, (0, 2))
    top[...] = top_in[...]
    total[...] = total_in[...]
    acc[...] = acc_in[...]
    for copy in copies:
        copy.wait()
    forward_pairs(
        count, q_ref, kband, vband, tile_of, place_of, (s0, m0), (s1, m1), top, total, acc
    )
    for tile in range(ROW_TILES):
        attended = acc[tile] / total[tile]
        flip_ref[tile] = attended.astype(BF)
        att_ref[tile] = attended.T.astype(BF)
        lse_ref[tile] = top[tile] + jnp.log2(total[tile])


def backward_pairs(
    count, q_ref, back, att_ref, lse_ref, kband, vband, tile_of, place_of,
    even, odd, delta, dk, dv, dq,
):
    for tile in range(ROW_TILES):
        prod = back[tile].astype(F32) * att_ref[tile].astype(F32)
        delta[tile] = jnp.sum(prod, axis=0, keepdims=True)

    def make(slot, i):
        tile, place = tile_of[i], place_of[i]
        scores = dot(kband[place], q_ref[tile], NT) * (SCALING * LOG2E)
        prob = jnp.exp2(scores - lse_ref[tile])
        prob_grad = dot(vband[place], back[tile], NN)
        slot[0][...] = prob.astype(BF)
        slot[1][...] = (prob * (prob_grad - delta[tile])).astype(BF)

    def use(slot, i):
        tile, place = tile_of[i], place_of[i]
        dv[place] += dot(slot[0][...], back[tile], NT)
        dk[place] += dot(slot[1][...], q_ref[tile], NN)
        dq[tile] += dot(kband[place], slot[1][...], TN)

    run_pairs(count, make, use, even, odd)


def backward_halo_kernel(
    pattern_ref, q_ref, back_mine_ref, back_got_ref, att_ref, lse_ref, above_ref, below_ref,
    early_ref,
    up_ref, down_ref, dq, back_ref, zero_ref,
    kband, vband, tile_of, place_of, p0, p1, d0, d1, delta, dk, dv, sem,
):
    copies = fill_band((above_ref, below_ref), kband, vband, sem)
    count = build_pairs(pattern_ref, tile_of, place_of, (0, 2))
    dk[...] = jnp.zeros(dk.shape, F32)
    dv[...] = jnp.zeros(dv.shape, F32)
    dq[...] = jnp.zeros(dq.shape, F32)
    zero_ref[...] = jnp.zeros(zero_ref.shape, F32)
    for tile in range(ROW_TILES):
        cols = pl.ds(tile * TILE, TILE)
        back_ref[tile] = (back_mine_ref[:, cols] + back_got_ref[:, cols].astype(F32)).astype(BF)
    for copy in copies:
        copy.wait()
    backward_pairs(
        count, q_ref, back_ref, att_ref, lse_ref, kband, vband, tile_of, place_of,
        (p0, d0), (p1, d1), delta, dk, dv, dq,
    )
    for i in range(ROW_TILES):
        up_ref[0, i] = dk[i].astype(BF)
        up_ref[1, i] = dv[i].astype(BF)
        down_ref[0, i] = dk[ROW_TILES + i].astype(BF)
        down_ref[1, i] = dv[ROW_TILES + i].astype(BF)


def backward_own_kernel(
    pattern_ref, q_ref, back_ref, att_ref, lse_ref, k_ref, v_ref, dq_in, early_ref,
    dq_ref, dk, dv, zero_ref,
    tile_of, place_of, p0, p1, d0, d1, delta, dq,
):
    count = build_pairs(pattern_ref, tile_of, place_of, (1,))
    dk[...] = jnp.zeros(dk.shape, F32)
    dv[...] = jnp.zeros(dv.shape, F32)
    zero_ref[...] = jnp.zeros(zero_ref.shape, F32)
    dq[...] = dq_in[...]
    backward_pairs(
        count, q_ref, back_ref, att_ref, lse_ref, k_ref, v_ref, tile_of, place_of,
        (p0, d0), (p1, d1), delta, dk, dv, dq,
    )
    for tile in range(ROW_TILES):
        dq_ref[tile] = (dq[tile] * SCALING).T.astype(BF)


def made_kernel(array_ref, zero_ref):
    zero_ref[...] = jnp.zeros(zero_ref.shape, F32)


def weight_kernel(place_ref, grad_ref, att_ref, other_ref, early_ref, send_ref, keep_ref, heads, total):
    half, core = place_ref[0], place_ref[1]
    heads[:, pl.ds(pl.multiple_of(half * HDIM, HDIM), HDIM)] = att_ref[...]
    heads[:, pl.ds(pl.multiple_of((1 - half) * HDIM, HDIM), HDIM)] = other_ref[...]
    total[...] = dot(grad_ref[...], heads[...], NN)
    rows = send_ref.shape[3]
    for low in range(2):
        for xh in range(2):
            chunk = low * 4 + xh * 2
            mine = pl.ds(pl.multiple_of((chunk + core) * rows, 8), rows)
            yours = pl.ds(pl.multiple_of((chunk + 1 - core) * rows, 8), rows)
            for a in range(2):
                lanes = slice(a * HDIM, (a + 1) * HDIM)
                keep_ref[a, low, xh] = total[mine, lanes]
                send_ref[a, low, xh] = total[yours, lanes].astype(BF)


VM = pl.BlockSpec(memory_space=pltpu.VMEM)
SM = pl.BlockSpec(memory_space=pltpu.SMEM)
HB = pl.BlockSpec(memory_space=pltpu.HBM)
BLOCK = (ROW_TILES, TILE, HDIM)
FLIP = (ROW_TILES, HDIM, TILE)
LINE = (ROW_TILES, 1, TILE)
HALO = (2 * ROW_TILES, TILE, HDIM)
PAIR_LISTS = [pltpu.SMEM((49,), jnp.int32), pltpu.SMEM((49,), jnp.int32)]
HALO_BAND = [pltpu.VMEM(HALO, BF), pltpu.VMEM(HALO, BF)]
SCORES = [pltpu.VMEM((TILE, TILE), F32)] * 2 + [pltpu.VMEM((1, TILE), F32)] * 2
TERMS = [pltpu.VMEM((TILE, TILE), BF)] * 4
DMA_SEMS = pltpu.SemaphoreType.DMA((4,))


def kernel_call(kernel, name, outs, in_specs, scratch, flops):
    return pl.pallas_call(
        kernel,
        name=name,
        out_shape=tuple(jax.ShapeDtypeStruct(shape, kind) for shape, kind in outs),
        in_specs=in_specs,
        out_specs=(VM,) * len(outs),
        scratch_shapes=scratch,
        compiler_params=pltpu.CompilerParams(vmem_limit_bytes=32 * 1024 * 1024),
        cost_estimate=pl.CostEstimate(
            flops=flops, bytes_accessed=4_000_000, transcendentals=3_000_000
        ),
    )


def forward_own(*args):
    return kernel_call(
        forward_own_kernel, "forward_own", [(LINE, F32), (LINE, F32), (FLIP, F32)],
        [SM, VM, VM, VM], PAIR_LISTS + SCORES, 3_000_000_000,
    )(*args)


def forward_halo(*args):
    state = [pltpu.VMEM(LINE, F32), pltpu.VMEM(LINE, F32), pltpu.VMEM(FLIP, F32)]
    return kernel_call(
        forward_halo_kernel, "forward_halo", [(BLOCK, BF), (FLIP, BF), (LINE, F32)],
        [SM] + [VM] * 4 + [HB] * 3, HALO_BAND + PAIR_LISTS + SCORES + state + [DMA_SEMS],
        5_000_000_000,
    )(*args)


def backward_halo(*args):
    outs = [((2,) + BLOCK, BF), ((2,) + BLOCK, BF), (FLIP, F32), (FLIP, BF), ((1, HDIM), F32)]
    return kernel_call(
        backward_halo_kernel, "backward_halo", outs, [SM] + [VM] * 5 + [HB] * 3,
        HALO_BAND + PAIR_LISTS + TERMS
        + [pltpu.VMEM(LINE, F32), pltpu.VMEM(HALO, F32), pltpu.VMEM(HALO, F32), DMA_SEMS],
        12_000_000_000,
    )(*args)


def backward_own(*args):
    outs = [(BLOCK, BF), (BLOCK, F32), (BLOCK, F32), ((1, HDIM), F32)]
    return kernel_call(
        backward_own_kernel, "backward_own", outs, [SM] + [VM] * 7 + [HB],
        PAIR_LISTS + TERMS + [pltpu.VMEM(LINE, F32), pltpu.VMEM(FLIP, F32)],
        6_000_000_000,
    )(*args)


def made(array):
    any_space = pl.BlockSpec(memory_space=pl.ANY)
    return kernel_call(made_kernel, "made", [((1, HDIM), F32)], [any_space], [], 1000)(array)[0]


def weight_parts(place, grad_half, att, att_other, early):
    feats, tokens = grad_half.shape
    shape = (2, 2, 2, feats // 8, HDIM)
    return kernel_call(
        weight_kernel, "weight_parts", [(shape, BF), (shape, F32)], [SM] + [VM] * 3 + [HB],
        [pltpu.VMEM((tokens, 2 * HDIM), BF), pltpu.VMEM((feats, 2 * HDIM), F32)],
        2_000_000_000,
    )(place, grad_half, att, att_other, early)


def shifted(block, distance):
    route = [(i - distance, i) for i in range(16) if 0 <= i - distance < 16]
    return lax.ppermute(block, ST, route)


def swapped(block):
    return lax.ppermute(block, "xl", [(0, 1), (1, 0)])


def halved(part, axis, distance, size, dim, bit):
    route = [(i, i ^ distance) for i in range(size)]
    send = lax.dynamic_index_in_dim(part, 1 - bit, dim, keepdims=False).astype(BF)
    keep = lax.dynamic_index_in_dim(part, bit, dim, keepdims=False)
    return keep, lax.ppermute(send, axis, route)


def body(queries, key_rows, value_rows, out_grad, proj_weight, pattern):
    half, y = lax.axis_index("xl"), lax.axis_index("y")
    tokens = queries.shape[1]
    place = jnp.stack((half, lax.axis_index("core"))).astype(jnp.int32)
    q = queries.reshape(BLOCK)
    keys, values = key_rows.reshape(BLOCK), value_rows.reshape(BLOCK)
    kv = jnp.stack((keys, values))
    above, below = shifted(kv, 1), shifted(kv, -1)

    grad_half = lax.all_gather(out_grad[0].T, "z", axis=0, tiled=True)
    feats = grad_half.shape[0]
    w_mine = lax.dynamic_slice_in_dim(proj_weight, half * feats, feats, 1)
    w_other = swapped(lax.dynamic_slice_in_dim(proj_weight, (1 - half) * feats, feats, 1))

    own_state = forward_own(pattern, q, keys, values)
    attended, att_flip, lse = forward_halo(pattern, q, *own_state, above, below, w_other)
    att = attended.reshape(tokens, HDIM)
    att_other = swapped(att)

    back_sent = dot(w_other, grad_half, NN).astype(BF)
    back_got = swapped(back_sent)
    back_mine = dot(w_mine, grad_half, NN)

    by_rows = (((0,), (1,)), ((), ()))
    part = dot(w_mine, att, by_rows) + dot(w_other, att_other, by_rows)
    part = part + made(back_sent)[:, :1]
    projected = lax.psum_scatter(part.astype(BF), "z", scatter_dimension=0, tiled=True)
    projected = projected.T[None]

    sent, kept = weight_parts(place, grad_half, att, att_other, back_sent)
    got = lax.ppermute(sent, "core", [(0, 1), (1, 0)])
    kept, got = halved(kept + got.astype(F32), "xh", 1, 2, 2, lax.axis_index("xh"))

    up, down, dq_part, back, _ = backward_halo(
        pattern, q, back_mine, back_got, att_flip, lse, above, below, sent
    )
    up, down = shifted(up, -1), shifted(down, 1)
    dq, dk, dv, zero = backward_own(pattern, q, back, att_flip, lse, keys, values, dq_part, kept)

    kept = (kept + got.astype(F32) + zero).astype(BF).reshape((4,) + kept.shape[2:])
    summed = 0.0
    for k in range(4):
        piece = lax.dynamic_index_in_dim(kept, y ^ k, 0, keepdims=False)
        route = [
            (h * 4 + i, (i ^ k) // 2 * 4 + 2 * h + (i ^ k) % 2) for h in range(2) for i in range(4)
        ]
        summed = summed + lax.ppermute(piece, ("xl", "y"), route).astype(F32)
    weight_grad = summed.T

    shape = (1, tokens, HDIM)
    key_grad = SCALING * (dk + up[0].astype(F32) + down[0].astype(F32))
    value_grad = dv + up[1].astype(F32) + down[1].astype(F32)
    key_grad = key_grad.astype(BF).reshape(shape)
    value_grad = value_grad.astype(BF).reshape(shape)
    return projected, dq.reshape(shape), key_grad, value_grad, weight_grad


def solution(mesh):
    fine = Mesh(mesh.devices.reshape(2, 8, 4, 2, 2), ("xl", "z", "y", "xh", "core"))
    fsdp = ("xl", "z")
    rows = P(None, ST, fsdp)
    return jax.shard_map(
        body,
        mesh=fine,
        in_specs=(rows, rows, rows, rows, P(fsdp, None), P(ST, None)),
        out_specs=(rows, rows, rows, rows, P(fsdp, ST)),
        check_vma=False,
    )
```

profile of v0, /device:TPU:99, one launch (start us, length us, event | category | flops | bytes accessed | tf_op | source)
XLA Modules:
  0.0 119.7 jit_solution(10603337978389395364)
XLA Ops:
  7.2 0.0 copy-start
  7.2 0.0 all-gather.2.cloned.1.call-start
  7.2 0.7 all-gather.2.cloned.1.call-update
  7.9 0.0 reduce-scatter.2.cloned.1.call-start
  8.0 1.2 pad_maximum_fusion
  9.2 2.6 %collective-permute-start.1 = (bf16[2,4,384,128]{3,2,1,0:T(8,128)(2,1)S(1)}, bf16[2,4,384,128]{3,2,1,0:T(8,128)(2,1)S(1)}, u32[]{:S(2)}, u32[]{:S(2)}) collective-permute-start(bf16[2,4,384,128]{3,2,1,0:T(8,128)(2,1)S(1)} %pad_maximum_fusion), channel_id=1, source_target_pairs={{1,0},{2,1},{3,2},{4,3},{5,4},{6,5},{7,6},{8,7},{9,8},{10,9},{11,1... | collective-permute-start | bytes 2359304 | tf_op jit(solution)/shard_map/ppermute | solution.py:305
  11.7 4.5 %collective-permute-start = (bf16[2,4,384,128]{3,2,1,0:T(8,128)(2,1)S(1)}, bf16[2,4,384,128]{3,2,1,0:T(8,128)(2,1)S(1)}, u32[]{:S(2)}, u32[]{:S(2)}) collective-permute-start(bf16[2,4,384,128]{3,2,1,0:T(8,128)(2,1)S(1)} %pad_maximum_fusion), channel_id=1, source_target_pairs={{0,1},{1,2},{2,3},{3,4},{4,5},{5,6},{6,7},{7,8},{8,9},{9,10},{10,1... | collective-permute-start | bytes 2359304 | tf_op jit(solution)/shard_map/ppermute | solution.py:305
  16.2 0.0 copy-done
  16.3 0.4 collective-permute-start.2
  16.7 1.0 copy-done.2
  17.7 1.0 copy-done.4
  18.7 1.0 copy-done.12
  19.7 0.7 copy-done.14
  20.4 3.2 %forward_own.1 = (f32[4,1,384]{2,1,0:T(1,128)S(1)}, f32[4,1,384]{2,1,0:T(1,128)S(1)}, f32[4,128,384]{2,1,0:T(8,128)S(1)}) custom-call(s32[4,27]{1,0:T(4,128)S(1)} %copy-done.14, bf16[4,384,128]{2,1,0:T(8,128)(2,1)S(1)} %bitcast.74, bf16[4,384,128]{2,1,0:T(8,128)(2,1)S(1)} %bitcast.67, bf16[4,384,128]{2,1,0:T(8,128)(2,1)S(1)} %bitcast.70), custom_call_target="tpu_custom_call" | custom-call | flops 3000000000 | bytes 4000000 | tf_op jit(solution)/shard_map/forward_own/pallas_call | solution.py:254
  23.6 7.1 %collective-permute-done.2.early_ref = bf16[128,768]{1,0:T(8,128)(2,1)S(1)} collective-permute-done((bf16[128,768]{1,0:T(8,128)(2,1)S(1)}, bf16[128,768]{1,0:T(8,128)(2,1)S(1)}, u32[]{:S(2)}, u32[]{:S(2)}) %collective-permute-start.2) | collective-permute-done | bytes 196640 | tf_op jit(solution)/shard_map/ppermute | solution.py:309
  30.7 0.0 collective-permute-done.1.below_ref
  30.7 0.0 collective-permute-done.above_ref
  30.7 0.0 copy-start.10
  30.7 7.1 %forward_halo.1 = (bf16[4,384,128]{2,1,0:T(8,128)(2,1)S(1)}, bf16[4,128,384]{2,1,0:T(8,128)(2,1)S(1)}, f32[4,1,384]{2,1,0:T(1,128)S(1)}) custom-call(s32[4,27]{1,0:T(4,128)S(1)} %copy-done.14, bf16[4,384,128]{2,1,0:T(8,128)(2,1)S(1)} %bitcast.75, f32[4,1,384]{2,1,0:T(1,128)S(1)} %get-tuple-element.21.top_in, f32[4,1,384]{2,1,0:T(1,128)S(1)} %get-tuple-element.22.total_in, ...), custom_call_target="tpu_custom_call" | custom-call | flops 5000000000 | bytes 4000000 | tf_op jit(solution)/shard_map/forward_halo/pallas_call | solution.py:262
  37.8 0.0 copy-done.8
  37.8 0.0 copy-done.10
  37.8 0.0 copy-start.16
  37.8 0.1 collective-permute-start.3
  37.9 11.1 %all-gather.2.cloned.1.call-done.grad_ref = bf16[768,1536]{1,0:T(8,128)(2,1)} async-done(((bf16[96,1536]{1,0:T(8,128)(2,1)}), bf16[768,1536]{1,0:T(8,128)(2,1)}) %all-gather.2.cloned.1.call-update) | async-done | bytes 2359312 | tf_op jit(solution)/shard_map/all_gather | solution.py:328
  49.0 2.1 %convolution_convert_fusion.array_ref.early_ref = bf16[128,1536]{1,0:T(8,128)(2,1)S(1)} fusion(bf16[128,768]{1,0:T(8,128)(2,1)S(1)} %collective-permute-done.2.early_ref, bf16[768,1536]{1,0:T(8,128)(2,1)} %all-gather.2.cloned.1.call-done.grad_ref), kind=kOutput, calls=%fused_computation.1 | convolution fusion | flops 302186496 | bytes 2949120 | tf_op jit(solution)/shard_map/dot_general | solution.py:28
  51.1 0.0 collective-permute-done.3.other_ref
  51.2 0.0 copy-start.6
  51.2 0.8 fusion.9
  52.0 2.3 %add_convert_fusion = bf16[768,1536]{1,0:T(8,128)(2,1)} fusion(f32[768,1536]{1,0:T(8,128)S(1)} %fusion.9, bf16[1536,128]{1,0:T(8,128)(2,1)S(1)} %bitcast.64, f32[]{:T(128)S(1)} %bitcast.73, bf16[128,1536]{1,0:T(8,128)(2,1)S(1)} %copy-done, s32[]{:T(128)S(6)} %select_n.26), kind=kOutput, calls=%fused_computation | convolution fusion | flops 305528832 | bytes 7668228 | tf_op jit(solution)/shard_map/dot_general | solution.py:28
  54.3 0.0 reduce-scatter.2.cloned.1.call-update
  54.4 0.1 pad_add_fusion.place_ref
  54.4 0.4 collective-permute-start.4
  54.8 1.2 copy-done.1
  56.0 1.0 copy-done.7
  57.0 1.5 %weight_parts.1 = (bf16[2,2,2,96,128]{4,3,2,1,0:T(8,128)(2,1)S(1)}, f32[2,2,2,96,128]{4,3,2,1,0:T(8,128)S(1)}) custom-call(s32[2]{0:T(128)S(1)} %pad_add_fusion.place_ref, bf16[768,1536]{1,0:T(8,128)(2,1)S(1)} %copy-done.1, bf16[1536,128]{1,0:T(8,128)(2,1)S(1)} %bitcast.65, bf16[1536,128]{1,0:T(8,128)(2,1)S(1)} %copy-done.7, ...), custom_call_target="tpu_custom_call" | custom-call | flops 2000000000 | bytes 4000000 | tf_op jit(solution)/shard_map/weight_parts/pallas_call | solution.py:296
  58.6 0.0 copy-start.13
  58.6 0.0 copy-start.15
  58.6 0.0 copy-start.17
  58.6 4.1 %collective-permute-start.5 = (bf16[2,2,2,96,128]{4,3,1,0,2:T(8,128)(2,1)S(1)}, bf16[2,2,2,96,128]{4,3,1,0,2:T(8,128)(2,1)S(1)}, u32[]{:S(2)}, u32[]{:S(2)}) collective-permute-start(bf16[2,2,2,96,128]{4,3,1,0,2:T(8,128)(2,1)S(1)} %copy.11), channel_id=1, source_target_pairs={{0,1},{1,0},{2,3},{3,2},{4,5},{5,4},{6,7},{7,6},{8,9},{9,8},{10,11... | collective-permute-start | bytes 589832 | tf_op jit(solution)/shard_map/ppermute | solution.py:349
  62.8 0.5 fusion.3.back_mine_ref
  63.2 0.6 collective-permute-done.5
  63.9 2.0 %collective-permute-start.8 = (bf16[2,2,96,128]{3,2,1,0:T(8,128)(2,1)S(1)}, bf16[2,2,96,128]{3,2,1,0:T(8,128)(2,1)S(1)}, u32[]{:S(2)}, u32[]{:S(2)}) collective-permute-start(bf16[2,2,96,128]{3,2,1,0:T(8,128)(2,1)S(1)} %fusion.6), channel_id=1, source_target_pairs={{0,2},{2,0},{1,3},{3,1},{4,6},{6,4},{5,7},{7,5},{8,10},{10,8},{9,1... | collective-permute-start | bytes 294920 | tf_op jit(solution)/shard_map/ppermute | solution.py:316
  65.9 0.0 collective-permute-done.4.back_got_ref
  66.0 0.0 copy-start.3
  66.0 0.0 copy-start.5
  66.0 10.9 %backward_halo.1 = (bf16[2,4,384,128]{3,2,1,0:T(8,128)(2,1)S(1)}, bf16[2,4,384,128]{3,2,1,0:T(8,128)(2,1)S(1)}, f32[4,128,384]{2,1,0:T(8,128)S(1)}, bf16[4,128,384]{2,1,0:T(8,128)(2,1)S(1)}, f32[1,128]{1,0:T(1,128)}) custom-call(s32[4,27]{1,0:T(4,128)S(1)} %copy-done.15, bf16[4,384,128]{2,1,0:T(8,128)(2,1)S(1)} %bitcast.76, ...), custom_call_target="tpu_custom_call" | custom-call | flops 12000000000 | bytes 4000000 | tf_op jit(solution)/shard_map/backward_halo/pallas_call | solution.py:271
  77.0 1.9 %collective-permute-start.6 = (bf16[2,4,384,128]{3,2,1,0:T(8,128)(2,1)S(1)}, bf16[2,4,384,128]{3,2,1,0:T(8,128)(2,1)S(1)}, u32[]{:S(2)}, u32[]{:S(2)}) collective-permute-start(bf16[2,4,384,128]{3,2,1,0:T(8,128)(2,1)S(1)} %get-tuple-element.33), channel_id=1, source_target_pairs={{1,0},{2,1},{3,2},{4,3},{5,4},{6,5},{7,6},{8,7},{9,8},{10,9},{11,1... | collective-permute-start | bytes 2359304 | tf_op jit(solution)/shard_map/ppermute | solution.py:305
  78.9 5.1 %collective-permute-start.7 = (bf16[2,4,384,128]{3,2,1,0:T(8,128)(2,1)S(1)}, bf16[2,4,384,128]{3,2,1,0:T(8,128)(2,1)S(1)}, u32[]{:S(2)}, u32[]{:S(2)}) collective-permute-start(bf16[2,4,384,128]{3,2,1,0:T(8,128)(2,1)S(1)} %get-tuple-element.34), channel_id=1, source_target_pairs={{0,1},{1,2},{2,3},{3,4},{4,5},{5,6},{6,7},{7,8},{8,9},{9,10},{10,1... | collective-permute-start | bytes 2359304 | tf_op jit(solution)/shard_map/ppermute | solution.py:305
  84.0 0.0 copy-done.3
  84.1 0.0 copy-done.5
  84.1 5.5 %backward_own.1 = (bf16[4,384,128]{2,1,0:T(8,128)(2,1)}, f32[4,384,128]{2,1,0:T(8,128)S(1)}, f32[4,384,128]{2,1,0:T(8,128)S(1)}, f32[1,128]{1,0:T(1,128)S(1)}) custom-call(s32[4,27]{1,0:T(4,128)S(1)} %copy-done.15, bf16[4,384,128]{2,1,0:T(8,128)(2,1)S(1)} %bitcast.77, bf16[4,128,384]{2,1,0:T(8,128)(2,1)S(1)} %get-tuple-element.28.back_ref, ...), custom_call_target="tpu_custom_call" | custom-call | flops 6000000000 | bytes 4000000 | tf_op jit(solution)/shard_map/backward_own/pallas_call | solution.py:281
  89.6 0.0 collective-permute-done.8
  89.7 9.2 %collective-permute-start.9 = (bf16[96,128]{1,0:T(8,128)(2,1)S(1)}, bf16[96,128]{1,0:T(8,128)(2,1)S(1)}, u32[]{:S(2)}, u32[]{:S(2)}) collective-permute-start(bf16[96,128]{1,0:T(8,128)(2,1)S(1)} %get-tuple-element.39), channel_id=1, source_target_pairs={{0,0},{4,4},{8,128},{12,132},{128,8},{132,12},{136,136},{140,140},... | collective-permute-start | bytes 73736 | tf_op jit(solution)/shard_map/ppermute | solution.py:365
  98.8 0.1 collective-permute-start.12
  98.9 5.3 %collective-permute-start.11 = (bf16[96,128]{1,0:T(8,128)(2,1)S(1)}, bf16[96,128]{1,0:T(8,128)(2,1)S(1)}, u32[]{:S(2)}, u32[]{:S(2)}) collective-permute-start(bf16[96,128]{1,0:T(8,128)(2,1)S(1)} %get-tuple-element.41), channel_id=1, source_target_pairs={{0,128},{4,132},{8,0},{12,4},{128,136},{132,140},{136,8},{140,12},... | collective-permute-start | bytes 73736 | tf_op jit(solution)/shard_map/ppermute | solution.py:365
  104.2 2.1 %collective-permute-done.9 = bf16[96,128]{1,0:T(8,128)(2,1)S(1)} collective-permute-done((bf16[96,128]{1,0:T(8,128)(2,1)S(1)}, bf16[96,128]{1,0:T(8,128)(2,1)S(1)}, u32[]{:S(2)}, u32[]{:S(2)}) %collective-permute-start.9) | collective-permute-done | bytes 24608 | tf_op jit(solution)/shard_map/ppermute | solution.py:365
  106.3 2.0 %collective-permute-start.10 = (bf16[96,128]{1,0:T(8,128)(2,1)S(1)}, bf16[96,128]{1,0:T(8,128)(2,1)S(1)}, u32[]{:S(2)}, u32[]{:S(2)}) collective-permute-start(bf16[96,128]{1,0:T(8,128)(2,1)S(1)} %get-tuple-element.42), channel_id=1, source_target_pairs={{0,4},{4,0},{8,132},{12,128},{128,12},{132,8},{136,140},{140,136},... | collective-permute-start | bytes 73736 | tf_op jit(solution)/shard_map/ppermute | solution.py:365
  108.2 0.0 collective-permute-done.12
  108.2 0.0 collective-permute-done.11
  108.2 2.8 %collective-permute-done.10 = bf16[96,128]{1,0:T(8,128)(2,1)S(1)} collective-permute-done((bf16[96,128]{1,0:T(8,128)(2,1)S(1)}, bf16[96,128]{1,0:T(8,128)(2,1)S(1)}, u32[]{:S(2)}, u32[]{:S(2)}) %collective-permute-start.10) | collective-permute-done | bytes 24608 | tf_op jit(solution)/shard_map/ppermute | solution.py:365
  111.1 0.6 add_bitcast_fusion
  111.7 0.0 collective-permute-done.6
  111.7 0.0 collective-permute-done.7
  111.7 1.2 fusion
  (25 shorter events, 0.2 us)
Async XLA Ops:
  7.2 9.1 %copy-start = (bf16[128,1536]{1,0:T(8,128)(2,1)S(1)}, bf16[128,1536]{1,0:T(8,128)(2,1)}, u32[]{:S(2)}) copy-start(bf16[128,1536]{1,0:T(8,128)(2,1)} %param.10) | copy-start | bytes 1179652
  7.2 41.8 %all-gather.2.cloned.1.call-start = ((), (), s32[]{:S(2)}) async-start(), calls=%async_computation.1 | async-start | bytes 2654208 | tf_op jit(solution)/shard_map/all_gather | solution.py:328
  7.9 105.0 %reduce-scatter.2.cloned.1.call-start = ((), (), s32[]{:S(2)}) async-start(), calls=%async_computation.2 | async-start | bytes 2654208 | tf_op jit(solution)/shard_map/reduce_scatter | solution.py:345
  9.2 21.5 %collective-permute-start.1 = (bf16[2,4,384,128]{3,2,1,0:T(8,128)(2,1)S(1)}, bf16[2,4,384,128]{3,2,1,0:T(8,128)(2,1)S(1)}, u32[]{:S(2)}, u32[]{:S(2)}) collective-permute-start(bf16[2,4,384,128]{3,2,1,0:T(8,128)(2,1)S(1)} %pad_maximum_fusion), channel_id=1, source_target_pairs={{1,0},{2,1},{3,2},{4,3},{5,4},{6,5},{7,6},{8,7},{9,8},{10,9},{11,1... | collective-permute-start | bytes 2359304 | tf_op jit(solution)/shard_map/ppermute | solution.py:305
  11.7 18.9 %collective-permute-start = (bf16[2,4,384,128]{3,2,1,0:T(8,128)(2,1)S(1)}, bf16[2,4,384,128]{3,2,1,0:T(8,128)(2,1)S(1)}, u32[]{:S(2)}, u32[]{:S(2)}) collective-permute-start(bf16[2,4,384,128]{3,2,1,0:T(8,128)(2,1)S(1)} %pad_maximum_fusion), channel_id=1, source_target_pairs={{0,1},{1,2},{2,3},{3,4},{4,5},{5,6},{6,7},{7,8},{8,9},{9,10},{10,1... | collective-permute-start | bytes 2359304 | tf_op jit(solution)/shard_map/ppermute | solution.py:305
  16.3 14.4 %collective-permute-start.2 = (bf16[128,768]{1,0:T(8,128)(2,1)S(1)}, bf16[128,768]{1,0:T(8,128)(2,1)S(1)}, u32[]{:S(2)}, u32[]{:S(2)}) collective-permute-start(bf16[128,768]{1,0:T(8,128)(2,1)S(1)} %constant_dynamic-slice_fusion), channel_id=1, source_target_pairs={{0,128},{128,0},{1,129},{129,1},{2,130},{130,2},{3,131},{131,3},{4... | collective-permute-start | bytes 589832 | tf_op jit(solution)/shard_map/ppermute | solution.py:309
  16.7 1.0 copy-start.2
  17.7 1.0 copy-start.4
  18.7 1.0 copy-start.12
  19.7 0.7 copy-start.14
  30.7 7.1 %copy-start.8 = (bf16[2,4,384,128]{3,2,1,0:T(8,128)(2,1)}, bf16[2,4,384,128]{3,2,1,0:T(8,128)(2,1)S(1)}, u32[]{:S(2)}) copy-start(bf16[2,4,384,128]{3,2,1,0:T(8,128)(2,1)S(1)} %collective-permute-done.1.below_ref) | copy-start | bytes 2359300
  30.7 7.1 %copy-start.10 = (bf16[2,4,384,128]{3,2,1,0:T(8,128)(2,1)}, bf16[2,4,384,128]{3,2,1,0:T(8,128)(2,1)S(1)}, u32[]{:S(2)}) copy-start(bf16[2,4,384,128]{3,2,1,0:T(8,128)(2,1)S(1)} %collective-permute-done.above_ref) | copy-start | bytes 2359300
  37.8 14.2 %copy-start.16 = (bf16[4,128,384]{2,1,0:T(8,128)(2,1)}, bf16[4,128,384]{2,1,0:T(8,128)(2,1)S(1)}, u32[]{:S(2)}) copy-start(bf16[4,128,384]{2,1,0:T(8,128)(2,1)S(1)} %get-tuple-element.25.att_ref) | copy-start | bytes 1179652
  37.8 13.3 %collective-permute-start.3 = (bf16[1536,128]{1,0:T(8,128)(2,1)S(1)}, bf16[1536,128]{1,0:T(8,128)(2,1)S(1)}, u32[]{:S(2)}, u32[]{:S(2)}) collective-permute-start(bf16[1536,128]{1,0:T(8,128)(2,1)S(1)} %bitcast.63), channel_id=1, source_target_pairs={{0,128},{128,0},{1,129},{129,1},{2,130},{130,2},{3,131},{131,3},{4... | collective-permute-start | bytes 1179656 | tf_op jit(solution)/shard_map/ppermute | solution.py:309
  51.2 0.8 copy-start.6
  54.3 1.7 %copy-start.1 = (bf16[768,1536]{1,0:T(8,128)(2,1)S(1)}, bf16[768,1536]{1,0:T(8,128)(2,1)}, u32[]{:S(2)}) copy-start(bf16[768,1536]{1,0:T(8,128)(2,1)} %all-gather.2.cloned.1.call-done.grad_ref) | copy-start | bytes 7077892
  54.4 11.5 %collective-permute-start.4 = (bf16[128,1536]{1,0:T(8,128)(2,1)S(1)}, bf16[128,1536]{1,0:T(8,128)(2,1)S(1)}, u32[]{:S(2)}, u32[]{:S(2)}) collective-permute-start(bf16[128,1536]{1,0:T(8,128)(2,1)S(1)} %convolution_convert_fusion.array_ref.early_ref), channel_id=1, source_target_pairs={{0,128},{128,0},{1,129},{129,1},{2,130},{130,2},{3,131},{131,3},{4... | collective-permute-start | bytes 1179656 | tf_op jit(solution)/shard_map/ppermute | solution.py:309
  56.0 1.0 copy-start.7
  58.6 7.4 %copy-start.9 = (bf16[2,4,384,128]{3,2,1,0:T(8,128)(2,1)S(1)}, bf16[2,4,384,128]{3,2,1,0:T(8,128)(2,1)}, u32[]{:S(2)}) copy-start(bf16[2,4,384,128]{3,2,1,0:T(8,128)(2,1)} %copy-done.8) | copy-start | bytes 2359300
  58.6 7.4 %copy-start.11 = (bf16[2,4,384,128]{3,2,1,0:T(8,128)(2,1)S(1)}, bf16[2,4,384,128]{3,2,1,0:T(8,128)(2,1)}, u32[]{:S(2)}) copy-start(bf16[2,4,384,128]{3,2,1,0:T(8,128)(2,1)} %copy-done.10) | copy-start | bytes 2359300
  58.6 7.4 %copy-start.13 = (bf16[1,1536,128]{2,1,0:T(8,128)(2,1)S(1)}, bf16[1,1536,128]{2,1,0:T(8,128)(2,1)}, u32[]{:S(2)}) copy-start(bf16[1,1536,128]{2,1,0:T(8,128)(2,1)} %param.6) | copy-start | bytes 1179652
  58.6 7.4 %copy-start.15 = (s32[4,27]{1,0:T(4,128)S(1)}, s32[4,27]{1,0:T(4,128)}, u32[]{:S(2)}) copy-start(s32[4,27]{1,0:T(4,128)} %pattern_ref.7) | copy-start | bytes 1300
  58.6 7.4 %copy-start.17 = (bf16[4,128,384]{2,1,0:T(8,128)(2,1)S(1)}, bf16[4,128,384]{2,1,0:T(8,128)(2,1)}, u32[]{:S(2)}) copy-start(bf16[4,128,384]{2,1,0:T(8,128)(2,1)} %copy-done.16) | copy-start | bytes 1179652
  58.6 5.2 %collective-permute-start.5 = (bf16[2,2,2,96,128]{4,3,1,0,2:T(8,128)(2,1)S(1)}, bf16[2,2,2,96,128]{4,3,1,0,2:T(8,128)(2,1)S(1)}, u32[]{:S(2)}, u32[]{:S(2)}) collective-permute-start(bf16[2,2,2,96,128]{4,3,1,0,2:T(8,128)(2,1)S(1)} %copy.11), channel_id=1, source_target_pairs={{0,1},{1,0},{2,3},{3,2},{4,5},{5,4},{6,7},{7,6},{8,9},{9,8},{10,11... | collective-permute-start | bytes 589832 | tf_op jit(solution)/shard_map/ppermute | solution.py:349
  63.9 25.7 %collective-permute-start.8 = (bf16[2,2,96,128]{3,2,1,0:T(8,128)(2,1)S(1)}, bf16[2,2,96,128]{3,2,1,0:T(8,128)(2,1)S(1)}, u32[]{:S(2)}, u32[]{:S(2)}) collective-permute-start(bf16[2,2,96,128]{3,2,1,0:T(8,128)(2,1)S(1)} %fusion.6), channel_id=1, source_target_pairs={{0,2},{2,0},{1,3},{3,1},{4,6},{6,4},{5,7},{7,5},{8,10},{10,8},{9,1... | collective-permute-start | bytes 294920 | tf_op jit(solution)/shard_map/ppermute | solution.py:316
  66.0 18.1 %copy-start.3 = (bf16[1,1536,128]{2,1,0:T(8,128)(2,1)S(1)}, bf16[1,1536,128]{2,1,0:T(8,128)(2,1)}, u32[]{:S(2)}) copy-start(bf16[1,1536,128]{2,1,0:T(8,128)(2,1)} %param.7) | copy-start | bytes 1179652
  66.0 18.0 %copy-start.5 = (bf16[1,1536,128]{2,1,0:T(8,128)(2,1)S(1)}, bf16[1,1536,128]{2,1,0:T(8,128)(2,1)}, u32[]{:S(2)}) copy-start(bf16[1,1536,128]{2,1,0:T(8,128)(2,1)} %param.8) | copy-start | bytes 1179652
  77.0 34.7 %collective-permute-start.6 = (bf16[2,4,384,128]{3,2,1,0:T(8,128)(2,1)S(1)}, bf16[2,4,384,128]{3,2,1,0:T(8,128)(2,1)S(1)}, u32[]{:S(2)}, u32[]{:S(2)}) collective-permute-start(bf16[2,4,384,128]{3,2,1,0:T(8,128)(2,1)S(1)} %get-tuple-element.33), channel_id=1, source_target_pairs={{1,0},{2,1},{3,2},{4,3},{5,4},{6,5},{7,6},{8,7},{9,8},{10,9},{11,1... | collective-permute-start | bytes 2359304 | tf_op jit(solution)/shard_map/ppermute | solution.py:305
  78.9 32.8 %collective-permute-start.7 = (bf16[2,4,384,128]{3,2,1,0:T(8,128)(2,1)S(1)}, bf16[2,4,384,128]{3,2,1,0:T(8,128)(2,1)S(1)}, u32[]{:S(2)}, u32[]{:S(2)}) collective-permute-start(bf16[2,4,384,128]{3,2,1,0:T(8,128)(2,1)S(1)} %get-tuple-element.34), channel_id=1, source_target_pairs={{0,1},{1,2},{2,3},{3,4},{4,5},{5,6},{6,7},{7,8},{8,9},{9,10},{10,1... | collective-permute-start | bytes 2359304 | tf_op jit(solution)/shard_map/ppermute | solution.py:305
  89.7 16.6 %collective-permute-start.9 = (bf16[96,128]{1,0:T(8,128)(2,1)S(1)}, bf16[96,128]{1,0:T(8,128)(2,1)S(1)}, u32[]{:S(2)}, u32[]{:S(2)}) collective-permute-start(bf16[96,128]{1,0:T(8,128)(2,1)S(1)} %get-tuple-element.39), channel_id=1, source_target_pairs={{0,0},{4,4},{8,128},{12,132},{128,8},{132,12},{136,136},{140,140},... | collective-permute-start | bytes 73736 | tf_op jit(solution)/shard_map/ppermute | solution.py:365
  98.8 9.4 %collective-permute-start.12 = (bf16[96,128]{1,0:T(8,128)(2,1)S(1)}, bf16[96,128]{1,0:T(8,128)(2,1)S(1)}, u32[]{:S(2)}, u32[]{:S(2)}) collective-permute-start(bf16[96,128]{1,0:T(8,128)(2,1)S(1)} %get-tuple-element.40), channel_id=1, source_target_pairs={{0,132},{4,128},{8,4},{12,0},{128,140},{132,136},{136,12},{140,8},... | collective-permute-start | bytes 73736 | tf_op jit(solution)/shard_map/ppermute | solution.py:365
  98.9 9.3 %collective-permute-start.11 = (bf16[96,128]{1,0:T(8,128)(2,1)S(1)}, bf16[96,128]{1,0:T(8,128)(2,1)S(1)}, u32[]{:S(2)}, u32[]{:S(2)}) collective-permute-start(bf16[96,128]{1,0:T(8,128)(2,1)S(1)} %get-tuple-element.41), channel_id=1, source_target_pairs={{0,128},{4,132},{8,0},{12,4},{128,136},{132,140},{136,8},{140,12},... | collective-permute-start | bytes 73736 | tf_op jit(solution)/shard_map/ppermute | solution.py:365
  106.3 4.8 %collective-permute-start.10 = (bf16[96,128]{1,0:T(8,128)(2,1)S(1)}, bf16[96,128]{1,0:T(8,128)(2,1)S(1)}, u32[]{:S(2)}, u32[]{:S(2)}) collective-permute-start(bf16[96,128]{1,0:T(8,128)(2,1)S(1)} %get-tuple-element.42), channel_id=1, source_target_pairs={{0,4},{4,0},{8,132},{12,128},{128,12},{132,8},{136,140},{140,136},... | collective-permute-start | bytes 73736 | tf_op jit(solution)/shard_map/ppermute | solution.py:365
Sparse Core Ops, SparseCore 0:
  9.8 39.1 all-gather.1
  54.5 41.5 reduce-scatter.1
where the time goes:
time: 120 us
  starting transfers between devices  37.7 us (31%)
  Pallas kernels  28.3 us (24%)
  waiting for transfers between devices  24.4 us (20%)
  between operations  14.4 us (12%)
  local copies, waits for them, and re-layouts  6 us (5%)
  matrix products  5.74 us (5%)
  other arithmetic  3.13 us (3%)
    ppermute x4, starting transfers between devices, body(): summed = summed + lax.ppermute(piece, ('xl', 'y'), route).astype(F32)  16.5 us
    ppermute x4, starting transfers between devices, shifted(): return lax.ppermute(block, ST, route)  14.1 us
    all_gather x1, waiting for transfers between devices, body(): grad_half = lax.all_gather(out_grad[0].T, 'z', axis=0, tiled=True)  11.1 us
    pallas_call x1, Pallas kernels, backward_halo(): kernel_call(backward_halo_kernel, 'backward_halo', outs, [SM] + [VM] * 5...  10.9 us
    ppermute x3, waiting for transfers between devices, swapped(): return lax.ppermute(block, 'xl', [(0, 1), (1, 0)])  7.13 us
    pallas_call x1, Pallas kernels, forward_halo(): kernel_call(forward_halo_kernel, 'forward_halo', [(BLOCK, BF), (FLIP, BF)...  7.09 us
    unnamed x36, local copies, waits for them, and re-layouts  5.91 us
    dot_general x4, matrix products, dot(): return lax.dot_general(a, b, dims, preferred_element_type=F32)  5.74 us
  transfers between devices with their start and end apart: 15, of which 5 were waited for; matrix products, arithmetic and copies ran while one was open for 5% of the time, Pallas kernels for 24%

commit v1 on v0

--- a/solution.py
+++ b/solution.py
@@ -200,7 +200,8 @@
         dq_ref[tile] = (dq[tile] * SCALING).T.astype(BF)
 
 
-def made_kernel(array_ref, zero_ref):
+def made_kernel(*refs):
+    zero_ref = refs[-1]
     zero_ref[...] = jnp.zeros(zero_ref.shape, F32)
 
 
@@ -285,9 +286,9 @@
     )(*args)
 
 
-def made(array):
+def made(*arrays):
     any_space = pl.BlockSpec(memory_space=pl.ANY)
-    return kernel_call(made_kernel, "made", [((1, HDIM), F32)], [any_space], [], 1000)(array)[0]
+    return kernel_call(made_kernel, "made", [((1, HDIM), F32)], [any_space] * len(arrays), [], 1000)(*arrays)[0]
 
 
 def weight_parts(place, grad_half, att, att_other, early):
@@ -339,15 +340,15 @@
     back_got = swapped(back_sent)
     back_mine = dot(w_mine, grad_half, NN)
 
-    by_rows = (((0,), (1,)), ((), ()))
-    part = dot(w_mine, att, by_rows) + dot(w_other, att_other, by_rows)
-    part = part + made(back_sent)[:, :1]
-    projected = lax.psum_scatter(part.astype(BF), "z", scatter_dimension=0, tiled=True)
-    projected = projected.T[None]
-
     sent, kept = weight_parts(place, grad_half, att, att_other, back_sent)
     got = lax.ppermute(sent, "core", [(0, 1), (1, 0)])
     kept, got = halved(kept + got.astype(F32), "xh", 1, 2, 2, lax.axis_index("xh"))
+
+    by_rows = (((0,), (1,)), ((), ()))
+    part = dot(w_mine, att, by_rows) + dot(w_other, att_other, by_rows)
+    part = part + made(back_got, kept)[:, :1]
+    projected = lax.psum_scatter(part.astype(BF), "z", scatter_dimension=0, tiled=True)
+    projected = projected.T[None]
 
     up, down, dq_part, back, _ = backward_halo(
         pattern, q, back_mine, back_got, att_flip, lse, above, below, sent

time: 120 us -> 123 us (1.025)
  the two profiles are of different devices: /device:TPU:99 before, /device:TPU:2 now
where the time goes in v1:
time: 123 us; the launch traced here: 120 us
  waiting for transfers between devices  33.8 us (27%)
  starting transfers between devices  33.5 us (27%)
  Pallas kernels  21.3 us (17%)
  between operations  14.4 us (12%)
  matrix products  6.9 us (6%)
  local copies, waits for them, and re-layouts  6.52 us (5%)
  other arithmetic  4.02 us (3%)
    all_gather x1, waiting for transfers between devices, body(): grad_half = lax.all_gather(out_grad[0].T, 'z', axis=0, tiled=True)  24.9 us
    ppermute x4, starting transfers between devices, body(): summed = summed + lax.ppermute(piece, ('xl', 'y'), route).astype(F32)  15.5 us
    ppermute x4, starting transfers between devices, shifted(): return lax.ppermute(block, ST, route)  11.8 us
    dot_general x4, matrix products, dot(): return lax.dot_general(a, b, dims, preferred_element_type=F32)  6.9 us
    unnamed x40, local copies, waits for them, and re-layouts  6.43 us
    pallas_call x1, Pallas kernels, backward_halo(): kernel_call(backward_halo_kernel, 'backward_halo', outs, [SM] + [VM] * 5...  6.28 us
    pallas_call x1, Pallas kernels, backward_own(): kernel_call(backward_own_kernel, 'backward_own', outs, [SM] + [VM] * 7 +...  5.57 us
    ppermute x4, waiting for transfers between devices, body(): summed = summed + lax.ppermute(piece, ('xl', 'y'), route).astype(F32)  5.24 us
  transfers between devices with their start and end apart: 15, of which 5 were waited for; matrix products, arithmetic and copies ran while one was open for 7% of the time, Pallas kernels for 18%

profile of v1, /device:TPU:2, one launch (start us, length us, event | category | flops | bytes accessed | tf_op | source)
XLA Modules:
  0.0 120.4 jit_solution(9261488023870237302)
XLA Ops:
  7.2 0.0 copy-start
  7.2 0.0 all-gather.2.cloned.1.call-start
  7.2 0.7 all-gather.2.cloned.1.call-update
  7.9 0.0 reduce-scatter.2.cloned.1.call-start
  8.0 2.1 %pad_maximum_fusion = bf16[2,4,384,128]{3,2,1,0:T(8,128)(2,1)} fusion(bf16[1,4,384,128]{3,2,1,0:T(8,128)(2,1)} %bitcast.69, bf16[1,4,384,128]{3,2,1,0:T(8,128)(2,1)} %bitcast.66), kind=kLoop, calls=%fused_computation.2 | loop fusion | flops 393216 | bytes 1572864 | tf_op jit(solution)/shard_map/stack | solution.py:326
  10.0 1.3 %collective-permute-start.1 = (bf16[2,4,384,128]{3,2,1,0:T(8,128)(2,1)}, bf16[2,4,384,128]{3,2,1,0:T(8,128)(2,1)S(1)}, u32[]{:S(2)}, u32[]{:S(2)}) collective-permute-start(bf16[2,4,384,128]{3,2,1,0:T(8,128)(2,1)} %pad_maximum_fusion), channel_id=1, source_target_pairs={{1,0},{2,1},{3,2},{4,3},{5,4},{6,5},{7,6},{8,7},{9,8},{10,9},{11,1... | collective-permute-start | bytes 2359304 | tf_op jit(solution)/shard_map/ppermute | solution.py:306
  11.3 3.1 %collective-permute-start = (bf16[2,4,384,128]{3,2,1,0:T(8,128)(2,1)}, bf16[2,4,384,128]{3,2,1,0:T(8,128)(2,1)S(1)}, u32[]{:S(2)}, u32[]{:S(2)}) collective-permute-start(bf16[2,4,384,128]{3,2,1,0:T(8,128)(2,1)} %pad_maximum_fusion), channel_id=1, source_target_pairs={{0,1},{1,2},{2,3},{3,4},{4,5},{5,6},{6,7},{7,8},{8,9},{9,10},{10,1... | collective-permute-start | bytes 2359304 | tf_op jit(solution)/shard_map/ppermute | solution.py:306
  14.4 2.4 %collective-permute-start.2 = (bf16[128,768]{1,0:T(8,128)(2,1)S(1)}, bf16[128,768]{1,0:T(8,128)(2,1)S(1)}, u32[]{:S(2)}, u32[]{:S(2)}) collective-permute-start(bf16[128,768]{1,0:T(8,128)(2,1)S(1)} %constant_dynamic-slice_fusion), channel_id=1, source_target_pairs={{0,128},{128,0},{1,129},{129,1},{2,130},{130,2},{3,131},{131,3},{4... | collective-permute-start | bytes 589832 | tf_op jit(solution)/shard_map/ppermute | solution.py:310
  16.8 1.0 copy-done.2
  17.8 1.0 copy-done.4
  18.8 1.0 copy-done.10
  19.8 0.7 copy-done.14
  20.5 3.2 %forward_own.1 = (f32[4,1,384]{2,1,0:T(1,128)S(1)}, f32[4,1,384]{2,1,0:T(1,128)S(1)}, f32[4,128,384]{2,1,0:T(8,128)S(1)}) custom-call(s32[4,27]{1,0:T(4,128)S(1)} %copy-done.14, bf16[4,384,128]{2,1,0:T(8,128)(2,1)S(1)} %bitcast.74, bf16[4,384,128]{2,1,0:T(8,128)(2,1)S(1)} %bitcast.67, bf16[4,384,128]{2,1,0:T(8,128)(2,1)S(1)} %bitcast.70), custom_call_target="tpu_custom_call" | custom-call | flops 3000000000 | bytes 4000000 | tf_op jit(solution)/shard_map/forward_own/pallas_call | solution.py:255
  23.7 0.0 collective-permute-done.2.early_ref
  23.7 0.0 collective-permute-done.1.below_ref
  23.7 0.0 collective-permute-done.above_ref
  23.7 4.2 %forward_halo.1 = (bf16[4,384,128]{2,1,0:T(8,128)(2,1)S(1)}, bf16[4,128,384]{2,1,0:T(8,128)(2,1)S(1)}, f32[4,1,384]{2,1,0:T(1,128)S(1)}) custom-call(s32[4,27]{1,0:T(4,128)S(1)} %copy-done.14, bf16[4,384,128]{2,1,0:T(8,128)(2,1)S(1)} %bitcast.75, f32[4,1,384]{2,1,0:T(1,128)S(1)} %get-tuple-element.21.top_in, f32[4,1,384]{2,1,0:T(1,128)S(1)} %get-tuple-element.22.total_in, ...), custom_call_target="tpu_custom_call" | custom-call | flops 5000000000 | bytes 4000000 | tf_op jit(solution)/shard_map/forward_halo/pallas_call | solution.py:263
  27.9 0.0 copy-start.16
  28.0 0.7 copy-done.16
  28.7 0.8 collective-permute-start.3
  29.5 0.1 pad_add_fusion.place_ref
  29.6 24.9 %all-gather.2.cloned.1.call-done.grad_ref = bf16[768,1536]{1,0:T(8,128)(2,1)} async-done(((bf16[96,1536]{1,0:T(8,128)(2,1)}), bf16[768,1536]{1,0:T(8,128)(2,1)}) %all-gather.2.cloned.1.call-update) | async-done | bytes 2359312 | tf_op jit(solution)/shard_map/all_gather | solution.py:329
  54.5 2.3 %convolution_convert_fusion.early_ref = bf16[128,1536]{1,0:T(8,128)(2,1)S(1)} fusion(bf16[128,768]{1,0:T(8,128)(2,1)S(1)} %collective-permute-done.2.early_ref, bf16[768,1536]{1,0:T(8,128)(2,1)} %all-gather.2.cloned.1.call-done.grad_ref), kind=kOutput, calls=%fused_computation.1 | convolution fusion | flops 302186496 | bytes 2949120 | tf_op jit(solution)/shard_map/dot_general | solution.py:28
  56.8 0.6 collective-permute-start.4
  57.4 0.0 collective-permute-done.3.other_ref
  57.4 0.0 copy-done.1
  57.4 2.0 %weight_parts.1 = (bf16[2,2,2,96,128]{4,3,2,1,0:T(8,128)(2,1)S(1)}, f32[2,2,2,96,128]{4,3,2,1,0:T(8,128)S(1)}) custom-call(s32[2]{0:T(128)S(1)} %pad_add_fusion.place_ref, bf16[768,1536]{1,0:T(8,128)(2,1)S(1)} %copy-done.1, bf16[1536,128]{1,0:T(8,128)(2,1)S(1)} %bitcast.64, bf16[1536,128]{1,0:T(8,128)(2,1)} %collective-permute-done.3.other_ref, ...), custom_call_target="tpu_custom_call" | custom-call | flops 2000000000 | bytes 4000000 | tf_op jit(solution)/shard_map/weight_parts/pallas_call | solution.py:297
  59.5 0.1 collective-permute-start.5
  59.6 1.8 %fusion.12 = f32[768,1536]{1,0:T(8,128)S(1)} fusion(bf16[128,768]{1,0:T(8,128)(2,1)S(1)} %collective-permute-done.2.early_ref, bf16[1536,128]{1,0:T(8,128)(2,1)} %collective-permute-done.3.other_ref), kind=kOutput, calls=%fused_computation.32 | convolution fusion | flops 301989888 | bytes 5308416 | tf_op jit(solution)/shard_map/dot_general | solution.py:28
  61.4 0.0 collective-permute-done.5
  61.4 0.0 copy-start.18
  61.5 0.7 copy-done.18
  62.2 2.5 %collective-permute-done.4.refs_0_.back_got_ref = bf16[128,1536]{1,0:T(8,128)(2,1)S(1)} collective-permute-done((bf16[128,1536]{1,0:T(8,128)(2,1)S(1)}, bf16[128,1536]{1,0:T(8,128)(2,1)S(1)}, u32[]{:S(2)}, u32[]{:S(2)}) %collective-permute-start.4) | collective-permute-done | bytes 393248 | tf_op jit(solution)/shard_map/ppermute | solution.py:310
  64.7 0.7 copy-done.12
  65.4 2.3 %add_convert_fusion = bf16[768,1536]{1,0:T(8,128)(2,1)} fusion(f32[768,1536]{1,0:T(8,128)S(1)} %fusion.12, f32[]{:T(128)S(1)} %bitcast.73, bf16[1536,128]{1,0:T(8,128)(2,1)S(1)} %bitcast.65, bf16[128,1536]{1,0:T(8,128)(2,1)S(1)} %copy-done, s32[]{:T(128)S(6)} %select_n.26), kind=kOutput, calls=%fused_computation | convolution fusion | flops 305528832 | bytes 7668228 | tf_op jit(solution)/shard_map/dot_general | solution.py:28
  67.7 0.0 reduce-scatter.2.cloned.1.call-update
  67.8 0.0 copy-start.11
  67.8 0.0 copy-start.15
  67.8 0.0 copy-start.19
  67.8 0.0 copy-start.13
  67.9 0.0 copy-start.17
  67.9 0.5 fusion.3.back_mine_ref
  68.4 0.5 copy-done.19
  68.9 2.2 %collective-permute-start.8 = (bf16[2,2,96,128]{3,2,1,0:T(8,128)(2,1)S(1)}, bf16[2,2,96,128]{3,2,1,0:T(8,128)(2,1)S(1)}, u32[]{:S(2)}, u32[]{:S(2)}) collective-permute-start(bf16[2,2,96,128]{3,2,1,0:T(8,128)(2,1)S(1)} %fusion.9), channel_id=1, source_target_pairs={{0,2},{2,0},{1,3},{3,1},{4,6},{6,4},{5,7},{7,5},{8,10},{10,8},{9,1... | collective-permute-start | bytes 294920 | tf_op jit(solution)/shard_map/ppermute | solution.py:317
  71.1 0.0 copy-start.3
  71.2 0.0 copy-start.5
  71.2 6.3 %backward_halo.1 = (bf16[2,4,384,128]{3,2,1,0:T(8,128)(2,1)S(1)}, bf16[2,4,384,128]{3,2,1,0:T(8,128)(2,1)S(1)}, f32[4,128,384]{2,1,0:T(8,128)S(1)}, bf16[4,128,384]{2,1,0:T(8,128)(2,1)S(1)}, f32[1,128]{1,0:T(1,128)}) custom-call(s32[4,27]{1,0:T(4,128)S(1)} %copy-done.15, bf16[4,384,128]{2,1,0:T(8,128)(2,1)S(1)} %bitcast.76, ...), custom_call_target="tpu_custom_call" | custom-call | flops 12000000000 | bytes 4000000 | tf_op jit(solution)/shard_map/backward_halo/pallas_call | solution.py:272
  77.5 1.3 %collective-permute-start.6 = (bf16[2,4,384,128]{3,2,1,0:T(8,128)(2,1)S(1)}, bf16[2,4,384,128]{3,2,1,0:T(8,128)(2,1)S(1)}, u32[]{:S(2)}, u32[]{:S(2)}) collective-permute-start(bf16[2,4,384,128]{3,2,1,0:T(8,128)(2,1)S(1)} %get-tuple-element.33), channel_id=1, source_target_pairs={{1,0},{2,1},{3,2},{4,3},{5,4},{6,5},{7,6},{8,7},{9,8},{10,9},{11,1... | collective-permute-start | bytes 2359304 | tf_op jit(solution)/shard_map/ppermute | solution.py:306
  78.8 6.1 %collective-permute-start.7 = (bf16[2,4,384,128]{3,2,1,0:T(8,128)(2,1)S(1)}, bf16[2,4,384,128]{3,2,1,0:T(8,128)(2,1)S(1)}, u32[]{:S(2)}, u32[]{:S(2)}) collective-permute-start(bf16[2,4,384,128]{3,2,1,0:T(8,128)(2,1)S(1)} %get-tuple-element.34), channel_id=1, source_target_pairs={{0,1},{1,2},{2,3},{3,4},{4,5},{5,6},{6,7},{7,8},{8,9},{9,10},{10,1... | collective-permute-start | bytes 2359304 | tf_op jit(solution)/shard_map/ppermute | solution.py:306
  84.9 5.6 %backward_own.1 = (bf16[4,384,128]{2,1,0:T(8,128)(2,1)}, f32[4,384,128]{2,1,0:T(8,128)S(1)}, f32[4,384,128]{2,1,0:T(8,128)S(1)}, f32[1,128]{1,0:T(1,128)S(1)}) custom-call(s32[4,27]{1,0:T(4,128)S(1)} %copy-done.15, bf16[4,384,128]{2,1,0:T(8,128)(2,1)S(1)} %bitcast.77, bf16[4,128,384]{2,1,0:T(8,128)(2,1)S(1)} %get-tuple-element.29.back_ref, ...), custom_call_target="tpu_custom_call" | custom-call | flops 6000000000 | bytes 4000000 | tf_op jit(solution)/shard_map/backward_own/pallas_call | solution.py:282
  90.5 0.0 collective-permute-done.8
  90.6 8.9 %collective-permute-start.9 = (bf16[96,128]{1,0:T(8,128)(2,1)S(1)}, bf16[96,128]{1,0:T(8,128)(2,1)S(1)}, u32[]{:S(2)}, u32[]{:S(2)}) collective-permute-start(bf16[96,128]{1,0:T(8,128)(2,1)S(1)} %get-tuple-element.39), channel_id=1, source_target_pairs={{0,0},{4,4},{8,128},{12,132},{128,8},{132,12},{136,136},{140,140},... | collective-permute-start | bytes 73736 | tf_op jit(solution)/shard_map/ppermute | solution.py:366
  99.5 0.1 collective-permute-start.12
  99.6 4.5 %collective-permute-start.11 = (bf16[96,128]{1,0:T(8,128)(2,1)S(1)}, bf16[96,128]{1,0:T(8,128)(2,1)S(1)}, u32[]{:S(2)}, u32[]{:S(2)}) collective-permute-start(bf16[96,128]{1,0:T(8,128)(2,1)S(1)} %get-tuple-element.41), channel_id=1, source_target_pairs={{0,128},{4,132},{8,0},{12,4},{128,136},{132,140},{136,8},{140,12},... | collective-permute-start | bytes 73736 | tf_op jit(solution)/shard_map/ppermute | solution.py:366
  104.0 1.4 %collective-permute-done.9 = bf16[96,128]{1,0:T(8,128)(2,1)S(1)} collective-permute-done((bf16[96,128]{1,0:T(8,128)(2,1)S(1)}, bf16[96,128]{1,0:T(8,128)(2,1)S(1)}, u32[]{:S(2)}, u32[]{:S(2)}) %collective-permute-start.9) | collective-permute-done | bytes 24608 | tf_op jit(solution)/shard_map/ppermute | solution.py:366
  105.4 2.0 %collective-permute-start.10 = (bf16[96,128]{1,0:T(8,128)(2,1)S(1)}, bf16[96,128]{1,0:T(8,128)(2,1)S(1)}, u32[]{:S(2)}, u32[]{:S(2)}) collective-permute-start(bf16[96,128]{1,0:T(8,128)(2,1)S(1)} %get-tuple-element.42), channel_id=1, source_target_pairs={{0,4},{4,0},{8,132},{12,128},{128,12},{132,8},{136,140},{140,136},... | collective-permute-start | bytes 73736 | tf_op jit(solution)/shard_map/ppermute | solution.py:366
  107.4 0.0 collective-permute-done.12
  107.4 0.0 collective-permute-done.11
  107.4 3.9 %collective-permute-done.10 = bf16[96,128]{1,0:T(8,128)(2,1)S(1)} collective-permute-done((bf16[96,128]{1,0:T(8,128)(2,1)S(1)}, bf16[96,128]{1,0:T(8,128)(2,1)S(1)}, u32[]{:S(2)}, u32[]{:S(2)}) %collective-permute-start.10) | collective-permute-done | bytes 24608 | tf_op jit(solution)/shard_map/ppermute | solution.py:366
  111.3 0.6 add_bitcast_fusion
  112.0 0.0 collective-permute-done.6
  112.0 0.0 collective-permute-done.7
  112.0 1.2 fusion
  113.2 0.4 reduce-scatter.2.cloned.1.call-done
  (29 shorter events, 0.2 us)
Async XLA Ops:
  7.2 7.2 %copy-start = (bf16[128,1536]{1,0:T(8,128)(2,1)S(1)}, bf16[128,1536]{1,0:T(8,128)(2,1)}, u32[]{:S(2)}) copy-start(bf16[128,1536]{1,0:T(8,128)(2,1)} %param.10) | copy-start | bytes 1179652
  7.2 47.3 %all-gather.2.cloned.1.call-start = ((), (), s32[]{:S(2)}) async-start(), calls=%async_computation.1 | async-start | bytes 2654208 | tf_op jit(solution)/shard_map/all_gather | solution.py:329
  7.9 105.6 %reduce-scatter.2.cloned.1.call-start = ((), (), s32[]{:S(2)}) async-start(), calls=%async_computation.2 | async-start | bytes 2654208 | tf_op jit(solution)/shard_map/reduce_scatter | solution.py:350
  10.0 13.7 %collective-permute-start.1 = (bf16[2,4,384,128]{3,2,1,0:T(8,128)(2,1)}, bf16[2,4,384,128]{3,2,1,0:T(8,128)(2,1)S(1)}, u32[]{:S(2)}, u32[]{:S(2)}) collective-permute-start(bf16[2,4,384,128]{3,2,1,0:T(8,128)(2,1)} %pad_maximum_fusion), channel_id=1, source_target_pairs={{1,0},{2,1},{3,2},{4,3},{5,4},{6,5},{7,6},{8,7},{9,8},{10,9},{11,1... | collective-permute-start | bytes 2359304 | tf_op jit(solution)/shard_map/ppermute | solution.py:306
  11.3 12.4 %collective-permute-start = (bf16[2,4,384,128]{3,2,1,0:T(8,128)(2,1)}, bf16[2,4,384,128]{3,2,1,0:T(8,128)(2,1)S(1)}, u32[]{:S(2)}, u32[]{:S(2)}) collective-permute-start(bf16[2,4,384,128]{3,2,1,0:T(8,128)(2,1)} %pad_maximum_fusion), channel_id=1, source_target_pairs={{0,1},{1,2},{2,3},{3,4},{4,5},{5,6},{6,7},{7,8},{8,9},{9,10},{10,1... | collective-permute-start | bytes 2359304 | tf_op jit(solution)/shard_map/ppermute | solution.py:306
  14.4 9.2 %collective-permute-start.2 = (bf16[128,768]{1,0:T(8,128)(2,1)S(1)}, bf16[128,768]{1,0:T(8,128)(2,1)S(1)}, u32[]{:S(2)}, u32[]{:S(2)}) collective-permute-start(bf16[128,768]{1,0:T(8,128)(2,1)S(1)} %constant_dynamic-slice_fusion), channel_id=1, source_target_pairs={{0,128},{128,0},{1,129},{129,1},{2,130},{130,2},{3,131},{131,3},{4... | collective-permute-start | bytes 589832 | tf_op jit(solution)/shard_map/ppermute | solution.py:310
  16.8 1.0 copy-start.2
  17.8 1.0 copy-start.4
  18.8 1.0 copy-start.10
  19.8 0.7 copy-start.14
  23.7 4.2 %copy-start.6 = (bf16[2,4,384,128]{3,2,1,0:T(8,128)(2,1)}, bf16[2,4,384,128]{3,2,1,0:T(8,128)(2,1)S(1)}, u32[]{:S(2)}) copy-start(bf16[2,4,384,128]{3,2,1,0:T(8,128)(2,1)S(1)} %collective-permute-done.1.below_ref) | copy-start | bytes 2359300
  23.7 4.2 %copy-start.8 = (bf16[2,4,384,128]{3,2,1,0:T(8,128)(2,1)}, bf16[2,4,384,128]{3,2,1,0:T(8,128)(2,1)S(1)}, u32[]{:S(2)}) copy-start(bf16[2,4,384,128]{3,2,1,0:T(8,128)(2,1)S(1)} %collective-permute-done.above_ref) | copy-start | bytes 2359300
  27.9 0.7 copy-start.16
  28.7 28.7 %collective-permute-start.3 = (bf16[1536,128]{1,0:T(8,128)(2,1)S(1)}, bf16[1536,128]{1,0:T(8,128)(2,1)}, u32[]{:S(2)}, u32[]{:S(2)}) collective-permute-start(bf16[1536,128]{1,0:T(8,128)(2,1)S(1)} %bitcast.63), channel_id=1, source_target_pairs={{0,128},{128,0},{1,129},{129,1},{2,130},{130,2},{3,131},{131,3},{4... | collective-permute-start | bytes 1179656 | tf_op jit(solution)/shard_map/ppermute | solution.py:310
  54.5 2.9 %copy-start.1 = (bf16[768,1536]{1,0:T(8,128)(2,1)S(1)}, bf16[768,1536]{1,0:T(8,128)(2,1)}, u32[]{:S(2)}) copy-start(bf16[768,1536]{1,0:T(8,128)(2,1)} %all-gather.2.cloned.1.call-done.grad_ref) | copy-start | bytes 7077892
  56.8 7.9 %collective-permute-start.4 = (bf16[128,1536]{1,0:T(8,128)(2,1)S(1)}, bf16[128,1536]{1,0:T(8,128)(2,1)S(1)}, u32[]{:S(2)}, u32[]{:S(2)}) collective-permute-start(bf16[128,1536]{1,0:T(8,128)(2,1)S(1)} %convolution_convert_fusion.early_ref), channel_id=1, source_target_pairs={{0,128},{128,0},{1,129},{129,1},{2,130},{130,2},{3,131},{131,3},{4... | collective-permute-start | bytes 1179656 | tf_op jit(solution)/shard_map/ppermute | solution.py:310
  59.5 1.9 %collective-permute-start.5 = (bf16[2,2,2,96,128]{4,3,1,0,2:T(8,128)(2,1)S(1)}, bf16[2,2,2,96,128]{4,3,1,0,2:T(8,128)(2,1)S(1)}, u32[]{:S(2)}, u32[]{:S(2)}) collective-permute-start(bf16[2,2,2,96,128]{4,3,1,0,2:T(8,128)(2,1)S(1)} %copy.11), channel_id=1, source_target_pairs={{0,1},{1,0},{2,3},{3,2},{4,5},{5,4},{6,7},{7,6},{8,9},{9,8},{10,11... | collective-permute-start | bytes 589832 | tf_op jit(solution)/shard_map/ppermute | solution.py:344
  61.4 0.7 copy-start.18
  64.7 0.7 copy-start.12
  67.8 3.4 %copy-start.11 = (bf16[1,1536,128]{2,1,0:T(8,128)(2,1)S(1)}, bf16[1,1536,128]{2,1,0:T(8,128)(2,1)}, u32[]{:S(2)}) copy-start(bf16[1,1536,128]{2,1,0:T(8,128)(2,1)} %param.6) | copy-start | bytes 1179652
  67.8 3.3 %copy-start.15 = (s32[4,27]{1,0:T(4,128)S(1)}, s32[4,27]{1,0:T(4,128)}, u32[]{:S(2)}) copy-start(s32[4,27]{1,0:T(4,128)} %pattern_ref.7) | copy-start | bytes 1300
  67.8 1.0 copy-start.19
  67.8 3.3 %copy-start.7 = (bf16[2,4,384,128]{3,2,1,0:T(8,128)(2,1)S(1)}, bf16[2,4,384,128]{3,2,1,0:T(8,128)(2,1)}, u32[]{:S(2)}) copy-start(bf16[2,4,384,128]{3,2,1,0:T(8,128)(2,1)} %copy-done.6) | copy-start | bytes 2359300
  67.8 3.3 %copy-start.9 = (bf16[2,4,384,128]{3,2,1,0:T(8,128)(2,1)S(1)}, bf16[2,4,384,128]{3,2,1,0:T(8,128)(2,1)}, u32[]{:S(2)}) copy-start(bf16[2,4,384,128]{3,2,1,0:T(8,128)(2,1)} %copy-done.8) | copy-start | bytes 2359300
  67.8 3.3 %copy-start.13 = (bf16[128,1536]{1,0:T(8,128)(2,1)S(1)}, bf16[128,1536]{1,0:T(8,128)(2,1)}, u32[]{:S(2)}) copy-start(bf16[128,1536]{1,0:T(8,128)(2,1)} %copy-done.12) | copy-start | bytes 1179652
  67.9 3.3 %copy-start.17 = (bf16[4,128,384]{2,1,0:T(8,128)(2,1)S(1)}, bf16[4,128,384]{2,1,0:T(8,128)(2,1)}, u32[]{:S(2)}) copy-start(bf16[4,128,384]{2,1,0:T(8,128)(2,1)} %copy-done.16) | copy-start | bytes 1179652
  68.9 21.6 %collective-permute-start.8 = (bf16[2,2,96,128]{3,2,1,0:T(8,128)(2,1)S(1)}, bf16[2,2,96,128]{3,2,1,0:T(8,128)(2,1)S(1)}, u32[]{:S(2)}, u32[]{:S(2)}) collective-permute-start(bf16[2,2,96,128]{3,2,1,0:T(8,128)(2,1)S(1)} %fusion.9), channel_id=1, source_target_pairs={{0,2},{2,0},{1,3},{3,1},{4,6},{6,4},{5,7},{7,5},{8,10},{10,8},{9,1... | collective-permute-start | bytes 294920 | tf_op jit(solution)/shard_map/ppermute | solution.py:317
  71.1 13.8 %copy-start.3 = (bf16[1,1536,128]{2,1,0:T(8,128)(2,1)S(1)}, bf16[1,1536,128]{2,1,0:T(8,128)(2,1)}, u32[]{:S(2)}) copy-start(bf16[1,1536,128]{2,1,0:T(8,128)(2,1)} %param.7) | copy-start | bytes 1179652
  71.2 13.8 %copy-start.5 = (bf16[1,1536,128]{2,1,0:T(8,128)(2,1)S(1)}, bf16[1,1536,128]{2,1,0:T(8,128)(2,1)}, u32[]{:S(2)}) copy-start(bf16[1,1536,128]{2,1,0:T(8,128)(2,1)} %param.8) | copy-start | bytes 1179652
  77.5 34.5 %collective-permute-start.6 = (bf16[2,4,384,128]{3,2,1,0:T(8,128)(2,1)S(1)}, bf16[2,4,384,128]{3,2,1,0:T(8,128)(2,1)S(1)}, u32[]{:S(2)}, u32[]{:S(2)}) collective-permute-start(bf16[2,4,384,128]{3,2,1,0:T(8,128)(2,1)S(1)} %get-tuple-element.33), channel_id=1, source_target_pairs={{1,0},{2,1},{3,2},{4,3},{5,4},{6,5},{7,6},{8,7},{9,8},{10,9},{11,1... | collective-permute-start | bytes 2359304 | tf_op jit(solution)/shard_map/ppermute | solution.py:306
  78.8 33.2 %collective-permute-start.7 = (bf16[2,4,384,128]{3,2,1,0:T(8,128)(2,1)S(1)}, bf16[2,4,384,128]{3,2,1,0:T(8,128)(2,1)S(1)}, u32[]{:S(2)}, u32[]{:S(2)}) collective-permute-start(bf16[2,4,384,128]{3,2,1,0:T(8,128)(2,1)S(1)} %get-tuple-element.34), channel_id=1, source_target_pairs={{0,1},{1,2},{2,3},{3,4},{4,5},{5,6},{6,7},{7,8},{8,9},{9,10},{10,1... | collective-permute-start | bytes 2359304 | tf_op jit(solution)/shard_map/ppermute | solution.py:306
  90.6 14.8 %collective-permute-start.9 = (bf16[96,128]{1,0:T(8,128)(2,1)S(1)}, bf16[96,128]{1,0:T(8,128)(2,1)S(1)}, u32[]{:S(2)}, u32[]{:S(2)}) collective-permute-start(bf16[96,128]{1,0:T(8,128)(2,1)S(1)} %get-tuple-element.39), channel_id=1, source_target_pairs={{0,0},{4,4},{8,128},{12,132},{128,8},{132,12},{136,136},{140,140},... | collective-permute-start | bytes 73736 | tf_op jit(solution)/shard_map/ppermute | solution.py:366
  99.5 8.0 %collective-permute-start.12 = (bf16[96,128]{1,0:T(8,128)(2,1)S(1)}, bf16[96,128]{1,0:T(8,128)(2,1)S(1)}, u32[]{:S(2)}, u32[]{:S(2)}) collective-permute-start(bf16[96,128]{1,0:T(8,128)(2,1)S(1)} %get-tuple-element.40), channel_id=1, source_target_pairs={{0,132},{4,128},{8,4},{12,0},{128,140},{132,136},{136,12},{140,8},... | collective-permute-start | bytes 73736 | tf_op jit(solution)/shard_map/ppermute | solution.py:366
  99.6 7.9 %collective-permute-start.11 = (bf16[96,128]{1,0:T(8,128)(2,1)S(1)}, bf16[96,128]{1,0:T(8,128)(2,1)S(1)}, u32[]{:S(2)}, u32[]{:S(2)}) collective-permute-start(bf16[96,128]{1,0:T(8,128)(2,1)S(1)} %get-tuple-element.41), channel_id=1, source_target_pairs={{0,128},{4,132},{8,0},{12,4},{128,136},{132,140},{136,8},{140,12},... | collective-permute-start | bytes 73736 | tf_op jit(solution)/shard_map/ppermute | solution.py:366
  105.4 5.9 %collective-permute-start.10 = (bf16[96,128]{1,0:T(8,128)(2,1)S(1)}, bf16[96,128]{1,0:T(8,128)(2,1)S(1)}, u32[]{:S(2)}, u32[]{:S(2)}) collective-permute-start(bf16[96,128]{1,0:T(8,128)(2,1)S(1)} %get-tuple-element.42), channel_id=1, source_target_pairs={{0,4},{4,0},{8,132},{12,128},{128,12},{132,8},{136,140},{140,136},... | collective-permute-start | bytes 73736 | tf_op jit(solution)/shard_map/ppermute | solution.py:366
Sparse Core Ops, SparseCore 0:
  9.8 44.6 all-gather.1
  67.9 45.6 reduce-scatter.1

commit v2 on v0

--- a/solution.py
+++ b/solution.py
@@ -69,8 +69,8 @@
     copies = []
     for i, ref in enumerate(refs):
         place = pl.ds(i * ROW_TILES, ROW_TILES)
-        copies.append(pltpu.make_async_copy(ref.at[0], kband.at[place], sem.at[2 * i]))
-        copies.append(pltpu.make_async_copy(ref.at[1], vband.at[place], sem.at[2 * i + 1]))
+        copies.append(pltpu.make_async_copy(ref[0], kband.at[place], sem.at[2 * i]))
+        copies.append(pltpu.make_async_copy(ref[1], vband.at[place], sem.at[2 * i + 1]))
     for copy in copies:
         copy.start()
     return copies
@@ -108,11 +108,11 @@
 
 
 def forward_halo_kernel(
-    pattern_ref, q_ref, top_in, total_in, acc_in, above_ref, below_ref, early_ref,
+    pattern_ref, q_ref, top_in, total_in, acc_in, ka_ref, va_ref, kb_ref, vb_ref, early_ref,
     att_ref, flip_ref, lse_ref,
     kband, vband, tile_of, place_of, s0, s1, m0, m1, top, total, acc, sem,
 ):
-    copies = fill_band((above_ref, below_ref), kband, vband, sem)
+    copies = fill_band(((ka_ref, va_ref), (kb_ref, vb_ref)), kband, vband, sem)
     count = build_pairs(pattern_ref, tile_of, place_of, (0, 2))
     top[...] = top_in[...]
     total[...] = total_in[...]
@@ -155,12 +155,12 @@
 
 
 def backward_halo_kernel(
-    pattern_ref, q_ref, back_mine_ref, back_got_ref, att_ref, lse_ref, above_ref, below_ref,
+    pattern_ref, q_ref, back_mine_ref, back_got_ref, att_ref, lse_ref, ka_ref, va_ref, kb_ref, vb_ref,
     early_ref,
     up_ref, down_ref, dq, back_ref, zero_ref,
     kband, vband, tile_of, place_of, p0, p1, d0, d1, delta, dk, dv, sem,
 ):
-    copies = fill_band((above_ref, below_ref), kband, vband, sem)
+    copies = fill_band(((ka_ref, va_ref), (kb_ref, vb_ref)), kband, vband, sem)
     count = build_pairs(pattern_ref, tile_of, place_of, (0, 2))
     dk[...] = jnp.zeros(dk.shape, F32)
     dv[...] = jnp.zeros(dv.shape, F32)
@@ -261,7 +261,7 @@
     state = [pltpu.VMEM(LINE, F32), pltpu.VMEM(LINE, F32), pltpu.VMEM(FLIP, F32)]
     return kernel_call(
         forward_halo_kernel, "forward_halo", [(BLOCK, BF), (FLIP, BF), (LINE, F32)],
-        [SM] + [VM] * 4 + [HB] * 3, HALO_BAND + PAIR_LISTS + SCORES + state + [DMA_SEMS],
+        [SM] + [VM] * 4 + [HB] * 5, HALO_BAND + PAIR_LISTS + SCORES + state + [DMA_SEMS],
         5_000_000_000,
     )(*args)
 
@@ -269,7 +269,7 @@
 def backward_halo(*args):
     outs = [((2,) + BLOCK, BF), ((2,) + BLOCK, BF), (FLIP, F32), (FLIP, BF), ((1, HDIM), F32)]
     return kernel_call(
-        backward_halo_kernel, "backward_halo", outs, [SM] + [VM] * 5 + [HB] * 3,
+        backward_halo_kernel, "backward_halo", outs, [SM] + [VM] * 5 + [HB] * 5,
         HALO_BAND + PAIR_LISTS + TERMS
         + [pltpu.VMEM(LINE, F32), pltpu.VMEM(HALO, F32), pltpu.VMEM(HALO, F32), DMA_SEMS],
         12_000_000_000,
@@ -322,8 +322,8 @@
     place = jnp.stack((half, lax.axis_index("core"))).astype(jnp.int32)
     q = queries.reshape(BLOCK)
     keys, values = key_rows.reshape(BLOCK), value_rows.reshape(BLOCK)
-    kv = jnp.stack((keys, values))
-    above, below = shifted(kv, 1), shifted(kv, -1)
+    above = shifted(keys, 1), shifted(values, 1)
+    below = shifted(keys, -1), shifted(values, -1)
 
     grad_half = lax.all_gather(out_grad[0].T, "z", axis=0, tiled=True)
     feats = grad_half.shape[0]
@@ -331,7 +331,7 @@
     w_other = swapped(lax.dynamic_slice_in_dim(proj_weight, (1 - half) * feats, feats, 1))
 
     own_state = forward_own(pattern, q, keys, values)
-    attended, att_flip, lse = forward_halo(pattern, q, *own_state, above, below, w_other)
+    attended, att_flip, lse = forward_halo(pattern, q, *own_state, *above, *below, w_other)
     att = attended.reshape(tokens, HDIM)
     att_other = swapped(att)
 
@@ -350,7 +350,7 @@
     kept, got = halved(kept + got.astype(F32), "xh", 1, 2, 2, lax.axis_index("xh"))
 
     up, down, dq_part, back, _ = backward_halo(
-        pattern, q, back_mine, back_got, att_flip, lse, above, below, sent
+        pattern, q, back_mine, back_got, att_flip, lse, *above, *below, sent
     )
     up, down = shifted(up, -1), shifted(down, 1)
     dq, dk, dv, zero = backward_own(pattern, q, back, att_flip, lse, keys, values, dq_part, kept)

time: 120 us -> 120 us (level)
  the two profiles are of different devices: /device:TPU:99 before, /device:TPU:253 now
where the time goes in v2:
time: 120 us; the launch traced here: 119 us
  starting transfers between devices  40.6 us (34%)
  waiting for transfers between devices  30.5 us (25%)
  Pallas kernels  20.1 us (17%)
  between operations  14.6 us (12%)
  matrix products  5.72 us (5%)
  local copies, waits for them, and re-layouts  5.68 us (5%)
  other arithmetic  1.94 us (2%)
    ppermute x6, starting transfers between devices, shifted(): return lax.ppermute(block, ST, route)  19.2 us
    all_gather x1, waiting for transfers between devices, body(): grad_half = lax.all_gather(out_grad[0].T, 'z', axis=0, tiled=True)  18.1 us
    ppermute x4, starting transfers between devices, body(): summed = summed + lax.ppermute(piece, ('xl', 'y'), route).astype(F32)  13.5 us
    ppermute x4, waiting for transfers between devices, body(): summed = summed + lax.ppermute(piece, ('xl', 'y'), route).astype(F32)  11.1 us
    pallas_call x1, Pallas kernels, backward_halo(): kernel_call(backward_halo_kernel, 'backward_halo', outs, [SM] + [VM] * 5...  6.82 us
    dot_general x4, matrix products, dot(): return lax.dot_general(a, b, dims, preferred_element_type=F32)  5.72 us
    unnamed x44, local copies, waits for them, and re-layouts  5.58 us
    pallas_call x1, Pallas kernels, backward_own(): kernel_call(backward_own_kernel, 'backward_own', outs, [SM] + [VM] * 7 +...  4.61 us
  transfers between devices with their start and end apart: 17, of which 4 were waited for; matrix products, arithmetic and copies ran while one was open for 4% of the time, Pallas kernels for 17%

profile of v2, /device:TPU:253, one launch (start us, length us, event | category | flops | bytes accessed | tf_op | source)
XLA Modules:
  0.0 119.1 jit_solution(69645449052460320)
XLA Ops:
  7.2 0.0 copy-start
  7.2 0.0 all-gather.2.cloned.1.call-start
  7.2 0.7 all-gather.2.cloned.1.call-update
  7.9 0.0 reduce-scatter.2.cloned.1.call-start
  8.0 2.6 %collective-permute-start.2 = (bf16[4,384,128]{2,1,0:T(8,128)(2,1)}, bf16[4,384,128]{2,1,0:T(8,128)(2,1)S(1)}, u32[]{:S(2)}, u32[]{:S(2)}) collective-permute-start(bf16[4,384,128]{2,1,0:T(8,128)(2,1)} %bitcast.70), channel_id=1, source_target_pairs={{1,0},{2,1},{3,2},{4,3},{5,4},{6,5},{7,6},{8,7},{9,8},{10,9},{11,1... | collective-permute-start | bytes 1179656 | tf_op jit(solution)/shard_map/ppermute | solution.py:305
  10.6 1.3 %collective-permute-start = (bf16[4,384,128]{2,1,0:T(8,128)(2,1)}, bf16[4,384,128]{2,1,0:T(8,128)(2,1)S(1)}, u32[]{:S(2)}, u32[]{:S(2)}) collective-permute-start(bf16[4,384,128]{2,1,0:T(8,128)(2,1)} %bitcast.71), channel_id=1, source_target_pairs={{0,1},{1,2},{2,3},{3,4},{4,5},{5,6},{6,7},{7,8},{8,9},{9,10},{10,1... | collective-permute-start | bytes 1179656 | tf_op jit(solution)/shard_map/ppermute | solution.py:305
  11.9 3.1 %collective-permute-start.3 = (bf16[4,384,128]{2,1,0:T(8,128)(2,1)}, bf16[4,384,128]{2,1,0:T(8,128)(2,1)S(1)}, u32[]{:S(2)}, u32[]{:S(2)}) collective-permute-start(bf16[4,384,128]{2,1,0:T(8,128)(2,1)} %bitcast.74), channel_id=1, source_target_pairs={{1,0},{2,1},{3,2},{4,3},{5,4},{6,5},{7,6},{8,7},{9,8},{10,9},{11,1... | collective-permute-start | bytes 1179656 | tf_op jit(solution)/shard_map/ppermute | solution.py:305
  14.9 1.3 %collective-permute-start.1 = (bf16[4,384,128]{2,1,0:T(8,128)(2,1)}, bf16[4,384,128]{2,1,0:T(8,128)(2,1)S(1)}, u32[]{:S(2)}, u32[]{:S(2)}) collective-permute-start(bf16[4,384,128]{2,1,0:T(8,128)(2,1)} %bitcast.75), channel_id=1, source_target_pairs={{0,1},{1,2},{2,3},{3,4},{4,5},{5,6},{6,7},{7,8},{8,9},{9,10},{10,1... | collective-permute-start | bytes 1179656 | tf_op jit(solution)/shard_map/ppermute | solution.py:305
  16.3 1.3 %collective-permute-start.4 = (bf16[128,768]{1,0:T(8,128)(2,1)S(1)}, bf16[128,768]{1,0:T(8,128)(2,1)S(1)}, u32[]{:S(2)}, u32[]{:S(2)}) collective-permute-start(bf16[128,768]{1,0:T(8,128)(2,1)S(1)} %constant_dynamic-slice_fusion), channel_id=1, source_target_pairs={{0,128},{128,0},{1,129},{129,1},{2,130},{130,2},{3,131},{131,3},{4... | collective-permute-start | bytes 589832 | tf_op jit(solution)/shard_map/ppermute | solution.py:309
  17.6 1.0 copy-done.4
  18.6 1.0 copy-done.6
  19.6 1.0 copy-done.8
  20.6 0.7 copy-done.18
  21.3 2.6 %forward_own.1 = (f32[4,1,384]{2,1,0:T(1,128)S(1)}, f32[4,1,384]{2,1,0:T(1,128)S(1)}, f32[4,128,384]{2,1,0:T(8,128)S(1)}) custom-call(s32[4,27]{1,0:T(4,128)S(1)} %copy-done.18, bf16[4,384,128]{2,1,0:T(8,128)(2,1)S(1)} %bitcast.66, bf16[4,384,128]{2,1,0:T(8,128)(2,1)S(1)} %bitcast.72, bf16[4,384,128]{2,1,0:T(8,128)(2,1)S(1)} %bitcast.76), custom_call_target="tpu_custom_call" | custom-call | flops 3000000000 | bytes 4000000 | tf_op jit(solution)/shard_map/forward_own/pallas_call | solution.py:254
  23.9 0.0 collective-permute-done.4.early_ref
  23.9 0.0 collective-permute-done.2.kb_ref
  23.9 0.0 collective-permute-done.ka_ref
  23.9 0.0 copy-start.12
  23.9 0.0 collective-permute-done.3.vb_ref
  24.0 0.0 collective-permute-done.1.va_ref
  24.0 0.0 copy-start.16
  24.0 4.5 %forward_halo.1 = (bf16[4,384,128]{2,1,0:T(8,128)(2,1)S(1)}, bf16[4,128,384]{2,1,0:T(8,128)(2,1)S(1)}, f32[4,1,384]{2,1,0:T(1,128)S(1)}) custom-call(s32[4,27]{1,0:T(4,128)S(1)} %copy-done.18, bf16[4,384,128]{2,1,0:T(8,128)(2,1)S(1)} %bitcast.67, f32[4,1,384]{2,1,0:T(1,128)S(1)} %get-tuple-element.21.top_in, f32[4,1,384]{2,1,0:T(1,128)S(1)} %get-tuple-element.22.total_in, ...), custom_call_target="tpu_custom_call" | custom-call | flops 5000000000 | bytes 4000000 | tf_op jit(solution)/shard_map/forward_halo/pallas_call | solution.py:262
  28.5 0.0 copy-start.20
  28.6 0.5 collective-permute-start.5
  29.0 18.1 %all-gather.2.cloned.1.call-done.grad_ref = bf16[768,1536]{1,0:T(8,128)(2,1)} async-done(((bf16[96,1536]{1,0:T(8,128)(2,1)}), bf16[768,1536]{1,0:T(8,128)(2,1)}) %all-gather.2.cloned.1.call-update) | async-done | bytes 2359312 | tf_op jit(solution)/shard_map/all_gather | solution.py:328
  47.1 2.1 %convolution_convert_fusion.array_ref.early_ref = bf16[128,1536]{1,0:T(8,128)(2,1)S(1)} fusion(bf16[128,768]{1,0:T(8,128)(2,1)S(1)} %collective-permute-done.4.early_ref, bf16[768,1536]{1,0:T(8,128)(2,1)} %all-gather.2.cloned.1.call-done.grad_ref), kind=kOutput, calls=%fused_computation.1 | convolution fusion | flops 302186496 | bytes 2949120 | tf_op jit(solution)/shard_map/dot_general | solution.py:28
  49.3 0.0 collective-permute-done.5.other_ref
  49.3 0.8 fusion.9
  50.1 2.3 %add_convert_fusion = bf16[768,1536]{1,0:T(8,128)(2,1)} fusion(f32[768,1536]{1,0:T(8,128)S(1)} %fusion.9, bf16[1536,128]{1,0:T(8,128)(2,1)S(1)} %bitcast.62, f32[]{:T(128)S(1)} %bitcast.65, bf16[128,1536]{1,0:T(8,128)(2,1)S(1)} %copy-done, s32[]{:T(128)S(6)} %select_n.26), kind=kOutput, calls=%fused_computation | convolution fusion | flops 305528832 | bytes 7668228 | tf_op jit(solution)/shard_map/dot_general | solution.py:28
  52.4 0.0 reduce-scatter.2.cloned.1.call-update
  52.5 0.1 pad_add_fusion.place_ref
  52.6 0.7 collective-permute-start.6
  53.3 0.8 copy-done.1
  54.1 1.0 copy-done.3
  55.1 1.5 %weight_parts.1 = (bf16[2,2,2,96,128]{4,3,2,1,0:T(8,128)(2,1)S(1)}, f32[2,2,2,96,128]{4,3,2,1,0:T(8,128)S(1)}) custom-call(s32[2]{0:T(128)S(1)} %pad_add_fusion.place_ref, bf16[768,1536]{1,0:T(8,128)(2,1)S(1)} %copy-done.1, bf16[1536,128]{1,0:T(8,128)(2,1)S(1)} %bitcast.63, bf16[1536,128]{1,0:T(8,128)(2,1)S(1)} %copy-done.3, ...), custom_call_target="tpu_custom_call" | custom-call | flops 2000000000 | bytes 4000000 | tf_op jit(solution)/shard_map/weight_parts/pallas_call | solution.py:296
  56.7 0.0 copy-start.5
  56.7 0.0 copy-start.13
  56.7 0.0 copy-start.17
  56.7 0.0 copy-start.19
  56.7 0.0 copy-start.21
  56.8 4.2 %collective-permute-start.7 = (bf16[2,2,2,96,128]{4,3,1,0,2:T(8,128)(2,1)S(1)}, bf16[2,2,2,96,128]{4,3,1,0,2:T(8,128)(2,1)S(1)}, u32[]{:S(2)}, u32[]{:S(2)}) collective-permute-start(bf16[2,2,2,96,128]{4,3,1,0,2:T(8,128)(2,1)S(1)} %copy.11), channel_id=1, source_target_pairs={{0,1},{1,0},{2,3},{3,2},{4,5},{5,4},{6,7},{7,6},{8,9},{9,8},{10,11... | collective-permute-start | bytes 589832 | tf_op jit(solution)/shard_map/ppermute | solution.py:349
  60.9 0.5 fusion.3.back_mine_ref
  61.4 0.6 collective-permute-done.7
  62.1 1.2 collective-permute-start.10
  63.3 0.0 collective-permute-done.6.back_got_ref
  63.3 0.0 copy-start.7
  63.3 0.0 copy-start.9
  63.4 6.8 %backward_halo.1 = (bf16[2,4,384,128]{3,2,1,0:T(8,128)(2,1)S(1)}, bf16[2,4,384,128]{3,2,1,0:T(8,128)(2,1)S(1)}, f32[4,128,384]{2,1,0:T(8,128)S(1)}, bf16[4,128,384]{2,1,0:T(8,128)(2,1)S(1)}, f32[1,128]{1,0:T(1,128)}) custom-call(s32[4,27]{1,0:T(4,128)S(1)} %copy-done.19, bf16[4,384,128]{2,1,0:T(8,128)(2,1)S(1)} %bitcast.68, ...), custom_call_target="tpu_custom_call" | custom-call | flops 12000000000 | bytes 4000000 | tf_op jit(solution)/shard_map/backward_halo/pallas_call | solution.py:271
  70.2 9.6 %collective-permute-start.8 = (bf16[2,4,384,128]{3,2,1,0:T(8,128)(2,1)S(1)}, bf16[2,4,384,128]{3,2,1,0:T(8,128)(2,1)S(1)}, u32[]{:S(2)}, u32[]{:S(2)}) collective-permute-start(bf16[2,4,384,128]{3,2,1,0:T(8,128)(2,1)S(1)} %get-tuple-element.33), channel_id=1, source_target_pairs={{1,0},{2,1},{3,2},{4,3},{5,4},{6,5},{7,6},{8,7},{9,8},{10,9},{11,1... | collective-permute-start | bytes 2359304 | tf_op jit(solution)/shard_map/ppermute | solution.py:305
  79.8 1.3 %collective-permute-start.9 = (bf16[2,4,384,128]{3,2,1,0:T(8,128)(2,1)S(1)}, bf16[2,4,384,128]{3,2,1,0:T(8,128)(2,1)S(1)}, u32[]{:S(2)}, u32[]{:S(2)}) collective-permute-start(bf16[2,4,384,128]{3,2,1,0:T(8,128)(2,1)S(1)} %get-tuple-element.34), channel_id=1, source_target_pairs={{0,1},{1,2},{2,3},{3,4},{4,5},{5,6},{6,7},{7,8},{8,9},{9,10},{10,1... | collective-permute-start | bytes 2359304 | tf_op jit(solution)/shard_map/ppermute | solution.py:305
  81.2 4.6 %backward_own.1 = (bf16[4,384,128]{2,1,0:T(8,128)(2,1)}, f32[4,384,128]{2,1,0:T(8,128)S(1)}, f32[4,384,128]{2,1,0:T(8,128)S(1)}, f32[1,128]{1,0:T(1,128)S(1)}) custom-call(s32[4,27]{1,0:T(4,128)S(1)} %copy-done.19, bf16[4,384,128]{2,1,0:T(8,128)(2,1)S(1)} %bitcast.69, bf16[4,128,384]{2,1,0:T(8,128)(2,1)S(1)} %get-tuple-element.28.back_ref, ...), custom_call_target="tpu_custom_call" | custom-call | flops 6000000000 | bytes 4000000 | tf_op jit(solution)/shard_map/backward_own/pallas_call | solution.py:281
  85.8 0.0 collective-permute-done.10
  85.8 12.5 %collective-permute-start.11 = (bf16[96,128]{1,0:T(8,128)(2,1)S(1)}, bf16[96,128]{1,0:T(8,128)(2,1)S(1)}, u32[]{:S(2)}, u32[]{:S(2)}) collective-permute-start(bf16[96,128]{1,0:T(8,128)(2,1)S(1)} %get-tuple-element.39), channel_id=1, source_target_pairs={{0,0},{4,4},{8,128},{12,132},{128,8},{132,12},{136,136},{140,140},... | collective-permute-start | bytes 73736 | tf_op jit(solution)/shard_map/ppermute | solution.py:365
  98.4 0.1 collective-permute-start.14
  98.5 0.9 collective-permute-start.13
  99.3 6.3 %collective-permute-done.11 = bf16[96,128]{1,0:T(8,128)(2,1)S(1)} collective-permute-done((bf16[96,128]{1,0:T(8,128)(2,1)S(1)}, bf16[96,128]{1,0:T(8,128)(2,1)S(1)}, u32[]{:S(2)}, u32[]{:S(2)}) %collective-permute-start.11) | collective-permute-done | bytes 24608 | tf_op jit(solution)/shard_map/ppermute | solution.py:365
  105.7 0.0 collective-permute-start.12
  105.7 0.0 collective-permute-done.14
  105.7 0.0 collective-permute-done.13
  105.7 4.8 %collective-permute-done.12 = bf16[96,128]{1,0:T(8,128)(2,1)S(1)} collective-permute-done((bf16[96,128]{1,0:T(8,128)(2,1)S(1)}, bf16[96,128]{1,0:T(8,128)(2,1)S(1)}, u32[]{:S(2)}, u32[]{:S(2)}) %collective-permute-start.12) | collective-permute-done | bytes 24608 | tf_op jit(solution)/shard_map/ppermute | solution.py:365
  110.4 0.6 add_bitcast_fusion
  111.1 0.0 collective-permute-done.8
  111.1 0.0 collective-permute-done.9
  111.1 1.2 fusion
  (36 shorter events, 0.2 us)
Async XLA Ops:
  7.2 9.1 %copy-start = (bf16[128,1536]{1,0:T(8,128)(2,1)S(1)}, bf16[128,1536]{1,0:T(8,128)(2,1)}, u32[]{:S(2)}) copy-start(bf16[128,1536]{1,0:T(8,128)(2,1)} %param.10) | copy-start | bytes 1179652
  7.2 40.0 %all-gather.2.cloned.1.call-start = ((), (), s32[]{:S(2)}) async-start(), calls=%async_computation.1 | async-start | bytes 2654208 | tf_op jit(solution)/shard_map/all_gather | solution.py:328
  7.9 104.3 %reduce-scatter.2.cloned.1.call-start = ((), (), s32[]{:S(2)}) async-start(), calls=%async_computation.2 | async-start | bytes 2654208 | tf_op jit(solution)/shard_map/reduce_scatter | solution.py:345
  8.0 15.9 %collective-permute-start.2 = (bf16[4,384,128]{2,1,0:T(8,128)(2,1)}, bf16[4,384,128]{2,1,0:T(8,128)(2,1)S(1)}, u32[]{:S(2)}, u32[]{:S(2)}) collective-permute-start(bf16[4,384,128]{2,1,0:T(8,128)(2,1)} %bitcast.70), channel_id=1, source_target_pairs={{1,0},{2,1},{3,2},{4,3},{5,4},{6,5},{7,6},{8,7},{9,8},{10,9},{11,1... | collective-permute-start | bytes 1179656 | tf_op jit(solution)/shard_map/ppermute | solution.py:305
  10.6 13.4 %collective-permute-start = (bf16[4,384,128]{2,1,0:T(8,128)(2,1)}, bf16[4,384,128]{2,1,0:T(8,128)(2,1)S(1)}, u32[]{:S(2)}, u32[]{:S(2)}) collective-permute-start(bf16[4,384,128]{2,1,0:T(8,128)(2,1)} %bitcast.71), channel_id=1, source_target_pairs={{0,1},{1,2},{2,3},{3,4},{4,5},{5,6},{6,7},{7,8},{8,9},{9,10},{10,1... | collective-permute-start | bytes 1179656 | tf_op jit(solution)/shard_map/ppermute | solution.py:305
  11.9 12.1 %collective-permute-start.3 = (bf16[4,384,128]{2,1,0:T(8,128)(2,1)}, bf16[4,384,128]{2,1,0:T(8,128)(2,1)S(1)}, u32[]{:S(2)}, u32[]{:S(2)}) collective-permute-start(bf16[4,384,128]{2,1,0:T(8,128)(2,1)} %bitcast.74), channel_id=1, source_target_pairs={{1,0},{2,1},{3,2},{4,3},{5,4},{6,5},{7,6},{8,7},{9,8},{10,9},{11,1... | collective-permute-start | bytes 1179656 | tf_op jit(solution)/shard_map/ppermute | solution.py:305
  14.9 9.0 %collective-permute-start.1 = (bf16[4,384,128]{2,1,0:T(8,128)(2,1)}, bf16[4,384,128]{2,1,0:T(8,128)(2,1)S(1)}, u32[]{:S(2)}, u32[]{:S(2)}) collective-permute-start(bf16[4,384,128]{2,1,0:T(8,128)(2,1)} %bitcast.75), channel_id=1, source_target_pairs={{0,1},{1,2},{2,3},{3,4},{4,5},{5,6},{6,7},{7,8},{8,9},{9,10},{10,1... | collective-permute-start | bytes 1179656 | tf_op jit(solution)/shard_map/ppermute | solution.py:305
  16.3 7.6 %collective-permute-start.4 = (bf16[128,768]{1,0:T(8,128)(2,1)S(1)}, bf16[128,768]{1,0:T(8,128)(2,1)S(1)}, u32[]{:S(2)}, u32[]{:S(2)}) collective-permute-start(bf16[128,768]{1,0:T(8,128)(2,1)S(1)} %constant_dynamic-slice_fusion), channel_id=1, source_target_pairs={{0,128},{128,0},{1,129},{129,1},{2,130},{130,2},{3,131},{131,3},{4... | collective-permute-start | bytes 589832 | tf_op jit(solution)/shard_map/ppermute | solution.py:309
  17.6 1.0 copy-start.4
  18.6 1.0 copy-start.6
  19.6 1.0 copy-start.8
  20.6 0.7 copy-start.18
  23.9 4.6 %copy-start.10 = (bf16[4,384,128]{2,1,0:T(8,128)(2,1)}, bf16[4,384,128]{2,1,0:T(8,128)(2,1)S(1)}, u32[]{:S(2)}) copy-start(bf16[4,384,128]{2,1,0:T(8,128)(2,1)S(1)} %collective-permute-done.2.kb_ref) | copy-start | bytes 1179652
  23.9 4.6 %copy-start.12 = (bf16[4,384,128]{2,1,0:T(8,128)(2,1)}, bf16[4,384,128]{2,1,0:T(8,128)(2,1)S(1)}, u32[]{:S(2)}) copy-start(bf16[4,384,128]{2,1,0:T(8,128)(2,1)S(1)} %collective-permute-done.ka_ref) | copy-start | bytes 1179652
  24.0 4.6 %copy-start.14 = (bf16[4,384,128]{2,1,0:T(8,128)(2,1)}, bf16[4,384,128]{2,1,0:T(8,128)(2,1)S(1)}, u32[]{:S(2)}) copy-start(bf16[4,384,128]{2,1,0:T(8,128)(2,1)S(1)} %collective-permute-done.3.vb_ref) | copy-start | bytes 1179652
  24.0 4.6 %copy-start.16 = (bf16[4,384,128]{2,1,0:T(8,128)(2,1)}, bf16[4,384,128]{2,1,0:T(8,128)(2,1)S(1)}, u32[]{:S(2)}) copy-start(bf16[4,384,128]{2,1,0:T(8,128)(2,1)S(1)} %collective-permute-done.1.va_ref) | copy-start | bytes 1179652
  28.5 21.6 %copy-start.20 = (bf16[4,128,384]{2,1,0:T(8,128)(2,1)}, bf16[4,128,384]{2,1,0:T(8,128)(2,1)S(1)}, u32[]{:S(2)}) copy-start(bf16[4,128,384]{2,1,0:T(8,128)(2,1)S(1)} %get-tuple-element.25.att_ref) | copy-start | bytes 1179652
  28.6 20.7 %collective-permute-start.5 = (bf16[1536,128]{1,0:T(8,128)(2,1)S(1)}, bf16[1536,128]{1,0:T(8,128)(2,1)S(1)}, u32[]{:S(2)}, u32[]{:S(2)}) collective-permute-start(bf16[1536,128]{1,0:T(8,128)(2,1)S(1)} %bitcast.61), channel_id=1, source_target_pairs={{0,128},{128,0},{1,129},{129,1},{2,130},{130,2},{3,131},{131,3},{4... | collective-permute-start | bytes 1179656 | tf_op jit(solution)/shard_map/ppermute | solution.py:309
  49.3 0.8 copy-start.2
  52.4 1.7 %copy-start.1 = (bf16[768,1536]{1,0:T(8,128)(2,1)S(1)}, bf16[768,1536]{1,0:T(8,128)(2,1)}, u32[]{:S(2)}) copy-start(bf16[768,1536]{1,0:T(8,128)(2,1)} %all-gather.2.cloned.1.call-done.grad_ref) | copy-start | bytes 7077892
  52.6 10.7 %collective-permute-start.6 = (bf16[128,1536]{1,0:T(8,128)(2,1)S(1)}, bf16[128,1536]{1,0:T(8,128)(2,1)S(1)}, u32[]{:S(2)}, u32[]{:S(2)}) collective-permute-start(bf16[128,1536]{1,0:T(8,128)(2,1)S(1)} %convolution_convert_fusion.array_ref.early_ref), channel_id=1, source_target_pairs={{0,128},{128,0},{1,129},{129,1},{2,130},{130,2},{3,131},{131,3},{4... | collective-permute-start | bytes 1179656 | tf_op jit(solution)/shard_map/ppermute | solution.py:309
  54.1 1.0 copy-start.3
  56.7 6.6 %copy-start.5 = (bf16[1,1536,128]{2,1,0:T(8,128)(2,1)S(1)}, bf16[1,1536,128]{2,1,0:T(8,128)(2,1)}, u32[]{:S(2)}) copy-start(bf16[1,1536,128]{2,1,0:T(8,128)(2,1)} %param.6) | copy-start | bytes 1179652
  56.7 6.6 %copy-start.11 = (bf16[4,384,128]{2,1,0:T(8,128)(2,1)S(1)}, bf16[4,384,128]{2,1,0:T(8,128)(2,1)}, u32[]{:S(2)}) copy-start(bf16[4,384,128]{2,1,0:T(8,128)(2,1)} %copy-done.10) | copy-start | bytes 1179652
  56.7 6.6 %copy-start.13 = (bf16[4,384,128]{2,1,0:T(8,128)(2,1)S(1)}, bf16[4,384,128]{2,1,0:T(8,128)(2,1)}, u32[]{:S(2)}) copy-start(bf16[4,384,128]{2,1,0:T(8,128)(2,1)} %copy-done.12) | copy-start | bytes 1179652
  56.7 6.6 %copy-start.15 = (bf16[4,384,128]{2,1,0:T(8,128)(2,1)S(1)}, bf16[4,384,128]{2,1,0:T(8,128)(2,1)}, u32[]{:S(2)}) copy-start(bf16[4,384,128]{2,1,0:T(8,128)(2,1)} %copy-done.14) | copy-start | bytes 1179652
  56.7 6.6 %copy-start.17 = (bf16[4,384,128]{2,1,0:T(8,128)(2,1)S(1)}, bf16[4,384,128]{2,1,0:T(8,128)(2,1)}, u32[]{:S(2)}) copy-start(bf16[4,384,128]{2,1,0:T(8,128)(2,1)} %copy-done.16) | copy-start | bytes 1179652
  56.7 6.6 %copy-start.19 = (s32[4,27]{1,0:T(4,128)S(1)}, s32[4,27]{1,0:T(4,128)}, u32[]{:S(2)}) copy-start(s32[4,27]{1,0:T(4,128)} %pattern_ref.7) | copy-start | bytes 1300
  56.7 6.6 %copy-start.21 = (bf16[4,128,384]{2,1,0:T(8,128)(2,1)S(1)}, bf16[4,128,384]{2,1,0:T(8,128)(2,1)}, u32[]{:S(2)}) copy-start(bf16[4,128,384]{2,1,0:T(8,128)(2,1)} %copy-done.20) | copy-start | bytes 1179652
  56.8 5.2 %collective-permute-start.7 = (bf16[2,2,2,96,128]{4,3,1,0,2:T(8,128)(2,1)S(1)}, bf16[2,2,2,96,128]{4,3,1,0,2:T(8,128)(2,1)S(1)}, u32[]{:S(2)}, u32[]{:S(2)}) collective-permute-start(bf16[2,2,2,96,128]{4,3,1,0,2:T(8,128)(2,1)S(1)} %copy.11), channel_id=1, source_target_pairs={{0,1},{1,0},{2,3},{3,2},{4,5},{5,4},{6,7},{7,6},{8,9},{9,8},{10,11... | collective-permute-start | bytes 589832 | tf_op jit(solution)/shard_map/ppermute | solution.py:349
  62.1 23.7 %collective-permute-start.10 = (bf16[2,2,96,128]{3,2,1,0:T(8,128)(2,1)S(1)}, bf16[2,2,96,128]{3,2,1,0:T(8,128)(2,1)S(1)}, u32[]{:S(2)}, u32[]{:S(2)}) collective-permute-start(bf16[2,2,96,128]{3,2,1,0:T(8,128)(2,1)S(1)} %fusion.6), channel_id=1, source_target_pairs={{0,2},{2,0},{1,3},{3,1},{4,6},{6,4},{5,7},{7,5},{8,10},{10,8},{9,1... | collective-permute-start | bytes 294920 | tf_op jit(solution)/shard_map/ppermute | solution.py:316
  63.3 17.8 %copy-start.7 = (bf16[1,1536,128]{2,1,0:T(8,128)(2,1)S(1)}, bf16[1,1536,128]{2,1,0:T(8,128)(2,1)}, u32[]{:S(2)}) copy-start(bf16[1,1536,128]{2,1,0:T(8,128)(2,1)} %param.7) | copy-start | bytes 1179652
  63.3 17.8 %copy-start.9 = (bf16[1,1536,128]{2,1,0:T(8,128)(2,1)S(1)}, bf16[1,1536,128]{2,1,0:T(8,128)(2,1)}, u32[]{:S(2)}) copy-start(bf16[1,1536,128]{2,1,0:T(8,128)(2,1)} %param.8) | copy-start | bytes 1179652
  70.2 40.9 %collective-permute-start.8 = (bf16[2,4,384,128]{3,2,1,0:T(8,128)(2,1)S(1)}, bf16[2,4,384,128]{3,2,1,0:T(8,128)(2,1)S(1)}, u32[]{:S(2)}, u32[]{:S(2)}) collective-permute-start(bf16[2,4,384,128]{3,2,1,0:T(8,128)(2,1)S(1)} %get-tuple-element.33), channel_id=1, source_target_pairs={{1,0},{2,1},{3,2},{4,3},{5,4},{6,5},{7,6},{8,7},{9,8},{10,9},{11,1... | collective-permute-start | bytes 2359304 | tf_op jit(solution)/shard_map/ppermute | solution.py:305
  79.8 31.2 %collective-permute-start.9 = (bf16[2,4,384,128]{3,2,1,0:T(8,128)(2,1)S(1)}, bf16[2,4,384,128]{3,2,1,0:T(8,128)(2,1)S(1)}, u32[]{:S(2)}, u32[]{:S(2)}) collective-permute-start(bf16[2,4,384,128]{3,2,1,0:T(8,128)(2,1)S(1)} %get-tuple-element.34), channel_id=1, source_target_pairs={{0,1},{1,2},{2,3},{3,4},{4,5},{5,6},{6,7},{7,8},{8,9},{9,10},{10,1... | collective-permute-start | bytes 2359304 | tf_op jit(solution)/shard_map/ppermute | solution.py:305
  85.8 19.8 %collective-permute-start.11 = (bf16[96,128]{1,0:T(8,128)(2,1)S(1)}, bf16[96,128]{1,0:T(8,128)(2,1)S(1)}, u32[]{:S(2)}, u32[]{:S(2)}) collective-permute-start(bf16[96,128]{1,0:T(8,128)(2,1)S(1)} %get-tuple-element.39), channel_id=1, source_target_pairs={{0,0},{4,4},{8,128},{12,132},{128,8},{132,12},{136,136},{140,140},... | collective-permute-start | bytes 73736 | tf_op jit(solution)/shard_map/ppermute | solution.py:365
  98.4 7.3 %collective-permute-start.14 = (bf16[96,128]{1,0:T(8,128)(2,1)S(1)}, bf16[96,128]{1,0:T(8,128)(2,1)S(1)}, u32[]{:S(2)}, u32[]{:S(2)}) collective-permute-start(bf16[96,128]{1,0:T(8,128)(2,1)S(1)} %get-tuple-element.40), channel_id=1, source_target_pairs={{0,132},{4,128},{8,4},{12,0},{128,140},{132,136},{136,12},{140,8},... | collective-permute-start | bytes 73736 | tf_op jit(solution)/shard_map/ppermute | solution.py:365
  98.5 7.2 %collective-permute-start.13 = (bf16[96,128]{1,0:T(8,128)(2,1)S(1)}, bf16[96,128]{1,0:T(8,128)(2,1)S(1)}, u32[]{:S(2)}, u32[]{:S(2)}) collective-permute-start(bf16[96,128]{1,0:T(8,128)(2,1)S(1)} %get-tuple-element.41), channel_id=1, source_target_pairs={{0,128},{4,132},{8,0},{12,4},{128,136},{132,140},{136,8},{140,12},... | collective-permute-start | bytes 73736 | tf_op jit(solution)/shard_map/ppermute | solution.py:365
  105.7 4.8 %collective-permute-start.12 = (bf16[96,128]{1,0:T(8,128)(2,1)S(1)}, bf16[96,128]{1,0:T(8,128)(2,1)S(1)}, u32[]{:S(2)}, u32[]{:S(2)}) collective-permute-start(bf16[96,128]{1,0:T(8,128)(2,1)S(1)} %get-tuple-element.42), channel_id=1, source_target_pairs={{0,4},{4,0},{8,132},{12,128},{128,12},{132,8},{136,140},{140,136},... | collective-permute-start | bytes 73736 | tf_op jit(solution)/shard_map/ppermute | solution.py:365
Sparse Core Ops, SparseCore 0:
  9.8 37.2 all-gather.1
  52.6 40.6 reduce-scatter.1
